TPU v7x, 32 devices: a whole 2x2x4 slice. The times are simulated.
32 devices in a mesh: section: 4 (over y, x), tp: 8 (over z, core).
Axes of the slice: x: 2, y: 2, z: 4, core: 2. Of those that a mesh axis runs over, the one named last changes fastest.
Arguments:
- tokens: bfloat16 [64, 8192], P(None, 'tp'), may hold values from -6 to 6
- norm_gain: float32 [4, 8192], P('section'), may hold values from 0.1 to 1.9
- gate_weight: bfloat16 [4, 8192, 16384], P('section', None, 'tp'), may hold values from -0.09375 to 0.09375
- up_weight: bfloat16 [4, 8192, 16384], P('section', None, 'tp'), may hold values from -0.09375 to 0.09375
- gate_mask: int32 [4, 128, 256], P('section', None, 'tp'), may hold values 0 or 1
- up_mask: int32 [4, 128, 256], P('section', None, 'tp'), may hold values 0 or 1
- down_weight: bfloat16 [4, 16384, 8192], P('section', 'tp'), may hold values from -0.125 to 0.125
- down_mask: int32 [4, 256, 128], P('section', 'tp'), may hold values 0 or 1
- slot_order: int32 [4, 256], P('section', 'tp'), may hold values from 0 to 255, as said below
Outputs:
- received: bfloat16 [4, 64, 8192], P('section', None, 'tp')
Inputs may be any that keep to these rules, and one draw needn't show every extreme that they name: `slot_order`: for each section a permutation of the 256 hidden blocks. Slot k lies on tp device k // 32; block b is computed on tp device b // 32. The slots of tp device t take exactly 4 blocks from each of the tp devices t, t + 1, ..., t + 8 - 1 (mod 8) and none from others. `gate_mask`: 1 keeps a block, 0 prunes it. `up_mask`: 1 keeps a block, 0 prunes it. `down_mask`: 1 keeps a block, 0 prunes it.
All inputs are finite; a program needn't handle non-finite values.
Results may differ from a plain program's by a relative error of at most 0.014.
Values may be sent and summed in bfloat16 or wider, within the bound.
No kernel may reach another device: no remote copies, remote signals or barrier semaphores. Data moves between devices by JAX's collectives and lax.ppermute only.
A program may use at most 320 MiB of HBM per device.

v0:
```python
import functools

import jax
import jax.numpy as jnp
from jax import lax
from jax.experimental import pallas as pl
from jax.experimental.pallas import tpu as pltpu
from jax.sharding import PartitionSpec as P


def passed_along(block, axis, distance):
    devices = range(lax.axis_size(axis))
    route = [((i - distance) % len(devices), i) for i in devices]
    return lax.ppermute(block, axis, route)


def expand_mask(mask, width):
    return jnp.repeat(jnp.repeat(mask, width, axis=0), width, axis=1)


def masked(weight, mask, width):
    return weight * expand_mask(mask, width).astype(jnp.bfloat16)


def ring_body(
    tokens,
    norm_gain,
    gate_weight,
    up_weight,
    gate_mask,
    up_mask,
    down_weight,
    down_mask,
    slot_order,
):
    sections = lax.axis_size("section")
    tp_count = lax.axis_size("tp")
    section_pos = lax.axis_index("section")
    tp_pos = lax.axis_index("tp")
    width = gate_weight.shape[1] // gate_mask.shape[1]
    w_gate = masked(gate_weight[0], gate_mask[0], width)
    w_up = masked(up_weight[0], up_mask[0], width)
    w_down = masked(down_weight[0], down_mask[0], width)
    gain = norm_gain[0]
    my_blocks = slot_order[0]
    per_device = my_blocks.shape[0]
    row_count, own_cols = tokens.shape
    window = min(tp_count, per_device)
    capacity = per_device // window
    slot_ids = jnp.arange(capacity, dtype=jnp.int32)
    my_source = my_blocks // per_device
    my_offset = (my_source - tp_pos) % tp_count
    lanes = jnp.arange(per_device, dtype=jnp.int32)
    earlier = (my_source[None, :] == my_source[:, None]) & (lanes[None, :] < lanes[:, None])
    my_rank = jnp.sum(earlier.astype(jnp.int32), axis=1)
    send_lists = []
    for offset in range(window):
        if offset == 0:
            table_row = my_blocks
        else:
            table_row = passed_along(my_blocks, "tp", offset)
        row_source = table_row // per_device
        row_block = table_row % per_device
        from_me = (row_source == tp_pos).astype(jnp.int32)
        order_rank = jnp.cumsum(from_me) - 1
        picks = (from_me[None, :] == 1) & (order_rank[None, :] == slot_ids[:, None])
        send_lists.append(jnp.sum(jnp.where(picks, row_block[None, :], 0), axis=1))
    x_full = lax.all_gather(tokens, "tp", axis=1, tiled=True)
    saved = jnp.zeros((row_count, own_cols), jnp.bfloat16)
    for round_pos in range(sections):
        x_own = lax.dynamic_slice_in_dim(x_full, tp_pos * own_cols, own_cols, 1)
        widened = x_full.astype(jnp.float32)
        scale = lax.rsqrt(jnp.mean(widened * widened, axis=-1, keepdims=True) + 1e-05)
        normed = (widened * scale * gain).astype(jnp.bfloat16)
        gate = jnp.dot(normed, w_gate, preferred_element_type=jnp.float32)
        upper = jnp.dot(normed, w_up, preferred_element_type=jnp.float32)
        hidden = (jax.nn.silu(gate) * upper).astype(jnp.bfloat16)
        flat = (
            hidden.reshape(row_count, per_device, width)
            .transpose(1, 0, 2)
            .reshape(per_device, row_count * width)
        )
        arrivals = []
        for gather_offset in range(window):
            outgoing = flat[send_lists[gather_offset]]
            if gather_offset == 0:
                arrivals.append(outgoing)
            else:
                arrivals.append(passed_along(outgoing, "tp", tp_count - gather_offset))
        stacked = jnp.stack(arrivals)
        chosen = stacked[my_offset, my_rank]
        mine = (
            chosen.reshape(per_device, row_count, width)
            .transpose(1, 0, 2)
            .reshape(row_count, per_device * width)
        )
        partial_sum = jnp.dot(mine, w_down, preferred_element_type=jnp.float32)
        summed = lax.psum_scatter(partial_sum, "tp", scatter_dimension=1, tiled=True)
        y_own = (x_own.astype(jnp.float32) + summed).astype(jnp.bfloat16)
        got_own = passed_along(y_own, "section", 1)
        if round_pos + 1 < sections:
            x_full = lax.all_gather(got_own, "tp", axis=1, tiled=True)
        saved = jnp.where(section_pos == (round_pos + 1) % sections, got_own, saved)
    return saved[None]


BF = jnp.bfloat16
F32 = jnp.float32
VM = pl.BlockSpec(memory_space=pltpu.VMEM)
SM = pl.BlockSpec(memory_space=pltpu.SMEM)
HB = pl.BlockSpec(memory_space=pltpu.HBM)
MIB = 2**20


def place(load_pair, first, second):
    lanes = lax.broadcasted_iota(jnp.int32, (1, 128), 1)
    left = pltpu.roll(load_pair(first // 2), 64 * (first % 2), 1)
    right = pltpu.roll(load_pair(second // 2), 64 * (1 - second % 2), 1)
    return jnp.where(lanes < 64, left, right).astype(BF)


GU_TILE, DN_TILE = 512, 512
GU_SLOTS, DN_SLOTS = 3, 3
GU_SPLIT, DN_SPLIT = 512, 256
GU_PARTS = ((0, 4), (3,), (2, 1), (7, 6, 5), (3, 2, 1))
GU_HELD = (2, 1, 2, 3, 0)
DN_PARTS = ((5, 7), (1, 3), (4, 6, 0, 2))
DN_HELD = (4, 4, 0)
GU_LAST, GU_FIRST_ROUND = 3, 4
GU_BROUGHT, GU_STAYING = (0, 1, 2), (3,)


def chosen(options, nth):
    value = options[0]
    for i, option in enumerate(options[1:]):
        value = jnp.where(nth == i + 1, option, value)
    return value


def place_of(me, piece):
    return me ^ (piece // 4 + 2 * (piece % 4))


def gate_up_row(me, pieces, cols, tile):
    per = cols // GU_TILE
    row = place_of(me, chosen(pieces, tile // per)) * cols + (tile % per) * GU_TILE
    return pl.multiple_of(row, GU_TILE)


def down_col(me, pieces, cols, tile):
    per = cols // DN_TILE
    col = place_of(me, chosen(pieces, tile // per)) * cols + (tile % per) * DN_TILE
    return pl.multiple_of(col, DN_TILE)


def spread_of(start, blocks, columns, width):
    return (
        lax.broadcasted_iota(jnp.int32, (blocks, columns), 0)
        == (start + lax.broadcasted_iota(jnp.int32, (blocks, columns), 1)) // width
    ).astype(BF)


def masks_kernel(gm, um, dm, gain, gu_masks, dn_masks, gain_ref, gm_ref, um_ref, dm_ref, sem):
    pairs = ((gm, gm_ref), (um, um_ref), (dm, dm_ref), (gain, gain_ref))
    copies = [pltpu.make_async_copy(src, dst, sem.at[n]) for n, (src, dst) in enumerate(pairs)]
    for copy in copies:
        copy.start()
    hid = gu_masks.shape[2]
    blocks = gm_ref.shape[0]
    spread = spread_of(0, blocks, hid, hid // blocks)
    for copy in copies:
        copy.wait()
    for j, mask in enumerate((gm_ref, um_ref)):
        gu_masks[j] = lax.dot_general(
            mask[...].astype(F32).astype(BF),
            spread,
            (((0,), (0,)), ((), ())),
            preferred_element_type=F32,
        )
    per = hid // DN_TILE
    for start in range(0, dm_ref.shape[1], blocks):
        mask = dm_ref[:, start : start + blocks].astype(F32).astype(BF)
        wide = jnp.dot(mask, spread, preferred_element_type=F32)
        for i in range(per):
            dn_masks[start // blocks * per + i] = wide[:, i * DN_TILE : (i + 1) * DN_TILE]


def spread_masks(gate_mask, up_mask, down_mask, gain, hid, depth):
    operands = [
        pltpu.with_memory_space_constraint(x, pltpu.HBM)
        for x in (gate_mask, up_mask, down_mask, gain)
    ]
    return pl.pallas_call(
        masks_kernel,
        in_specs=[HB] * 4,
        out_specs=(VM, VM, VM),
        out_shape=(
            jax.ShapeDtypeStruct((2, gate_mask.shape[1], hid), F32),
            jax.ShapeDtypeStruct((depth // DN_TILE, down_mask.shape[0], DN_TILE), F32),
            jax.ShapeDtypeStruct(gain.shape, F32),
        ),
        scratch_shapes=[pltpu.VMEM(x.shape, jnp.int32) for x in operands[:3]]
        + [pltpu.SemaphoreType.DMA((4,))],
        compiler_params=pltpu.CompilerParams(vmem_limit_bytes=4 * MIB),
        name="spread_masks",
    )(*operands)


def owner_and_place(block, per_device):
    if per_device & (per_device - 1):
        return lax.div(block, per_device), lax.rem(block, per_device)
    return block >> (per_device.bit_length() - 1), block & (per_device - 1)


def slots_kernel(cols, per_device, order, me_ref, *refs):
    x_refs, refs = refs[: len(order)], refs[len(order) :]
    send_ref, take_ref, table, orders, sem, found, count = refs
    me = me_ref[0]
    for x_ref, places in zip(x_refs, order):
        for i, piece in enumerate(places):
            row = x_ref[i, pl.ds(0, 16), pl.ds(cols, 128)].astype(F32)[0:1]
            table[pl.ds(piece, 1), :] = row.astype(jnp.int32)
    copy = pltpu.make_async_copy(table, orders, sem)
    copy.start()
    copy.wait()
    pieces = orders.shape[0]
    capacity = per_device // pieces

    def send_body(slot, ranks):
        after = []
        for piece, rank in enumerate(ranks):
            block = orders[piece, slot]
            owner, at = owner_and_place(block, per_device)
            found[piece * (capacity + 1) + rank] = at
            after.append(rank + (owner == me).astype(jnp.int32))
        return tuple(after)

    lax.fori_loop(0, per_device, send_body, (jnp.int32(0),) * pieces, unroll=2)
    for piece in range(pieces):
        count[piece] = 0
        for rank in range(capacity):
            send_ref[piece * capacity + rank] = found[piece * (capacity + 1) + rank]

    def take_body(slot, carry):
        apart = owner_and_place(orders[0, slot], per_device)[0] ^ me
        piece = (apart & 1) * (pieces // 2) + (apart >> 1)
        rank = count[piece]
        take_ref[slot] = piece * capacity + rank
        count[piece] = rank + 1
        return carry

    lax.fori_loop(0, per_device, take_body, 0)


def slots(me, xs, order, cols, per_device):
    pieces = sum(len(places) for places in order)
    table = jax.ShapeDtypeStruct((per_device,), jnp.int32)
    return pl.pallas_call(
        functools.partial(slots_kernel, cols, per_device, order),
        in_specs=[SM] + [VM] * len(xs),
        out_specs=(SM, SM),
        out_shape=(table, table),
        scratch_shapes=[
            pltpu.VMEM((pieces, 128), jnp.int32),
            pltpu.SMEM((pieces, 128), jnp.int32),
            pltpu.SemaphoreType.DMA,
            pltpu.SMEM((per_device + pieces,), jnp.int32),
            pltpu.SMEM((pieces,), jnp.int32),
        ],
        compiler_params=pltpu.CompilerParams(vmem_limit_bytes=MIB),
        name="slots",
    )(me, *xs)


def hold_kernel(parts, me_ref, *refs):
    me = me_ref[0]
    sem = refs[-1]
    weights, held_refs = refs[: -1 - len(parts)], refs[-1 - len(parts) : -1]
    pairs = []
    for pieces, ref in zip(parts, held_refs):
        for tile in range(ref.shape[0]):
            if len(weights) == 2:
                row = gate_up_row(me, pieces, weights[0].shape[1] // 8, tile)
                for j, w in enumerate(weights):
                    pairs.append((w.at[0, pl.ds(row, GU_TILE)], ref.at[tile, j]))
            else:
                col = down_col(me, pieces, weights[0].shape[2] // 8, tile)
                pairs.append((weights[0].at[0, :, pl.ds(col, DN_TILE)], ref.at[tile]))
    copies = [pltpu.make_async_copy(src, dst, sem.at[n]) for n, (src, dst) in enumerate(pairs)]
    for copy in copies:
        copy.start()
    for copy in copies:
        copy.wait()


def hold(parts, counts, me, weights):
    if len(weights) == 2:
        shapes = [(n, 2, GU_TILE, weights[0].shape[2]) for n in counts]
    else:
        shapes = [(n, weights[0].shape[1], DN_TILE) for n in counts]
    shapes = [jax.ShapeDtypeStruct(shape, BF) for shape in shapes]
    return pl.pallas_call(
        functools.partial(hold_kernel, parts),
        in_specs=[SM] + [HB] * len(weights),
        out_specs=(VM,) * len(shapes),
        out_shape=tuple(shapes),
        scratch_shapes=[pltpu.SemaphoreType.DMA((len(weights) * sum(counts),))],
        compiler_params=pltpu.CompilerParams(vmem_limit_bytes=2 * MIB),
        cost_estimate=pl.CostEstimate(
            flops=0, bytes_accessed=sum(2 * x.size for x in shapes), transcendentals=0
        ),
        name="hold",
    )(me, *weights)


def held_parts(parts, me, w_gate, w_up):
    return hold(
        tuple(GU_PARTS[part] for part in parts),
        tuple(GU_HELD[part] for part in parts),
        me,
        (w_gate, w_up),
    )


def gate_up_kernel(part, n_x, n_before, n_held, me_ref, send_ref, gain_ref, masks, *refs):
    pieces = GU_PARTS[part]
    last = part == GU_LAST
    x_refs, refs = refs[:n_x], refs[n_x:]
    before, refs = refs[: 2 * n_before], refs[2 * n_before :]
    if n_held:
        held, refs = refs[0], refs[1:]
    wg, wu = refs[:2]
    if last:
        out_ref, buf, sem, scaled, acc = refs[2:]
    else:
        acc, sq_ref, buf, sem, scaled = refs[2:]
    rows, cols = scaled.shape[1:]
    depth, hid = wg.shape[1:]
    width = depth // masks.shape[1]
    per = cols // GU_TILE
    kept = GU_TILE // width
    streamed = len(pieces) * per - n_held
    me = me_ref[0]

    def copies(nth, slot):
        row = gate_up_row(me, pieces, cols, n_held + nth)
        return [
            pltpu.make_async_copy(
                w.at[0, pl.ds(row, GU_TILE)], buf.at[slot, j], sem.at[slot, j]
            )
            for j, w in enumerate((wg, wu))
        ]

    slots = min(GU_SLOTS, streamed)
    for nth in range(slots):
        for copy in copies(nth, nth):
            copy.start()
    squares = jnp.zeros((rows, 128), F32)
    at = 0
    for x_ref in x_refs:
        for i in range(x_ref.shape[0]):
            start = pl.multiple_of(place_of(me, pieces[at]) * cols, cols)
            wide = x_ref[i, :, pl.ds(0, cols)].astype(F32)
            for lane in range(0, cols, 128):
                squares = squares + wide[:, lane : lane + 128] * wide[:, lane : lane + 128]
            scaled[at] = (wide * gain_ref[:, pl.ds(start, cols)]).astype(BF)
            at += 1
    if n_before:
        for j in range(2):
            total = before[0][j]
            for i in range(1, n_before):
                total = total + before[2 * i][j]
            acc[j] = total
        for i in range(n_before):
            squares = squares + before[2 * i + 1][...]
    else:
        acc[...] = jnp.zeros_like(acc)

    def add_product(tile, j, weight_ref):
        lanes = pl.ds(pl.multiple_of((tile % per) * GU_TILE, GU_TILE), GU_TILE)
        x_part = scaled[tile // per, :, lanes]
        row = gate_up_row(me, pieces, cols, tile)
        mask = masks[j, pl.ds(pl.multiple_of(row // width, kept), kept), :].astype(BF)
        for start in range(0, hid, GU_SPLIT):
            split = slice(start, start + GU_SPLIT)
            weight = weight_ref[:, split].reshape(kept, width, GU_SPLIT) * mask[:, None, split]
            acc[j, :, split] += jnp.dot(
                x_part, weight.reshape(GU_TILE, GU_SPLIT), preferred_element_type=F32
            )

    def step_body(with_held, nth, carry):
        slot = lax.rem(nth, slots)
        for j, copy in enumerate(copies(nth, slot)):
            if with_held:
                add_product(nth, j, held.at[nth, j])
            copy.wait()
            add_product(n_held + nth, j, buf.at[slot, j])

        @pl.when(nth + slots < streamed)
        def _():
            for copy in copies(nth + slots, slot):
                copy.start()

        return carry

    def held_body(nth, carry):
        for j in range(2):
            add_product(nth, j, held.at[nth, j])
        return carry

    both = min(n_held, streamed)
    if both < n_held:
        lax.fori_loop(both, n_held, held_body, 0)
    if both:
        lax.fori_loop(0, both, functools.partial(step_body, True), 0)
    if both < streamed:
        lax.fori_loop(both, streamed, functools.partial(step_body, False), 0)
    if not last:
        sq_ref[...] = squares
        return
    scale = lax.rsqrt(jnp.sum(squares, axis=1, keepdims=True) / depth + 1e-05)
    gate = acc[0] * scale
    hidden = (gate / (1.0 + jnp.exp(-gate)) * (acc[1] * scale)).astype(BF)
    acc[0] = hidden.astype(F32)

    def load_pair(pair):
        return acc[0, :, pl.ds(pl.multiple_of(pair * 128, 128), 128)]

    each = out_ref.shape[2] // 128
    for piece in range(out_ref.shape[0]):
        for pair in range(each):
            at = piece * 2 * each + 2 * pair
            out_ref[piece, :, pl.ds(pair * 128, 128)] = place(
                load_pair, send_ref[at], send_ref[at + 1]
            )


def gate_up(part, me, send, gain, masks, xs, before, held, w_gate, w_up):
    rows = xs[0].shape[1]
    depth, hid = w_gate.shape[1:]
    cols = depth // 8
    pieces = len(GU_PARTS[part])
    last = part == GU_LAST
    acc = (2, rows, hid)
    scratch = [
        pltpu.VMEM((GU_SLOTS, 2, GU_TILE, hid), BF),
        pltpu.SemaphoreType.DMA((GU_SLOTS, 2)),
        pltpu.VMEM((pieces, rows, cols), BF),
    ]
    if last:
        out_specs, out_shape = VM, jax.ShapeDtypeStruct((8, rows, hid // 8), BF)
        scratch.append(pltpu.VMEM(acc, F32))
    else:
        out_specs = (VM, VM)
        out_shape = (jax.ShapeDtypeStruct(acc, F32), jax.ShapeDtypeStruct((rows, 128), F32))
    operands = list(xs) + list(before) + list(held)
    n_held = held[0].shape[0] if held else 0
    return pl.pallas_call(
        functools.partial(gate_up_kernel, part, len(xs), len(before) // 2, n_held),
        in_specs=[SM, SM, VM, VM] + [VM] * len(operands) + [HB, HB],
        out_specs=out_specs,
        out_shape=out_shape,
        scratch_shapes=scratch,
        compiler_params=pltpu.CompilerParams(vmem_limit_bytes=15 * MIB),
        cost_estimate=pl.CostEstimate(
            flops=4 * rows * pieces * cols * hid,
            bytes_accessed=4 * (pieces * cols - n_held * GU_TILE) * hid,
            transcendentals=0,
        ),
        name="gate_up",
    )(me, send, gain, masks, *operands, w_gate, w_up)


def down_kernel(part, n_held, me_ref, take_ref, inner_ref, x_ref, masks, *refs):
    pieces = DN_PARTS[part]
    if n_held:
        held, refs = refs[0], refs[1:]
    wd, refs = refs[0], refs[1:]
    first, last = part == 0, part == len(DN_PARTS) - 1
    if first:
        out_ref, mine, buf, sem = refs
    elif last:
        out_ref, pass_ref, buf, sem = refs
    else:
        out_ref, buf, sem = refs
    if not first:
        mine = inner_ref
    hid, depth = wd.shape[1:]
    cols = depth // 8
    blocks = masks.shape[1]
    width = hid // blocks
    per = cols // DN_TILE
    streamed = len(pieces) * per - n_held
    n_slots = min(DN_SLOTS, streamed)
    me = me_ref[0]

    def copy_of(nth, slot):
        col = down_col(me, pieces, cols, n_held + nth)
        return pltpu.make_async_copy(wd.at[0, :, pl.ds(col, DN_TILE)], buf.at[slot], sem.at[slot])

    for nth in range(n_slots):
        copy_of(nth, nth).start()
    if first:
        each = inner_ref.shape[2] // 128

        def load_pair(pair):
            lane = pl.multiple_of((pair % each) * 128, 128)
            return inner_ref[pair // each, :, pl.ds(lane, 128)].astype(F32)

        for pair in range(hid // 128):
            mine[:, pl.ds(pair * 128, 128)] = place(
                load_pair, take_ref[2 * pair], take_ref[2 * pair + 1]
            )

    def put(tile, weight_ref):
        mask = masks[down_col(me, pieces, cols, tile) // DN_TILE].astype(BF)
        for start in range(0, DN_TILE, DN_SPLIT):
            split = slice(start, start + DN_SPLIT)
            weight = weight_ref[:, split].reshape(blocks, width, DN_SPLIT) * mask[:, None, split]
            result = jnp.dot(
                mine[...], weight.reshape(hid, DN_SPLIT), preferred_element_type=F32
            )
            lanes = pl.ds(pl.multiple_of((tile % per) * DN_TILE + start, DN_SPLIT), DN_SPLIT)
            out_ref[tile // per, :, lanes] = result.astype(out_ref.dtype)

    def held_body(nth, carry):
        put(nth, held.at[nth])
        return carry

    def step_body(with_held, nth, carry):
        slot = lax.rem(nth, n_slots)
        if with_held:
            put(nth, held.at[nth])
        copy_of(nth, slot).wait()
        put(n_held + nth, buf.at[slot])

        @pl.when(nth + n_slots < streamed)
        def _():
            copy_of(nth + n_slots, slot).start()

        return carry

    both = min(n_held, streamed)
    if both < n_held:
        lax.fori_loop(both, n_held, held_body, 0)
    if both:
        lax.fori_loop(0, both, functools.partial(step_body, True), 0)
    if both < streamed:
        lax.fori_loop(both, streamed, functools.partial(step_body, False), 0)
    if last:
        passed = pass_ref.shape[0]
        pass_ref[...] = out_ref[pl.ds(0, passed)].astype(BF)
        out_ref[passed] += x_ref[:, pl.ds(0, cols)].astype(F32)


def down(part, me, take, inner, x_own, masks, held, w_down):
    hid, depth = w_down.shape[1:]
    rows = x_own.shape[0]
    cols = depth // 8
    pieces = len(DN_PARTS[part])
    n_held = held[0].shape[0] if held else 0
    out = [jax.ShapeDtypeStruct((pieces, rows, cols), F32 if part else BF)]
    if part == 0:
        out.append(jax.ShapeDtypeStruct((rows, hid), BF))
    if part == len(DN_PARTS) - 1:
        out.append(jax.ShapeDtypeStruct((pieces // 2, rows, cols), BF))
    return pl.pallas_call(
        functools.partial(down_kernel, part, n_held),
        in_specs=[SM, SM, VM, VM, VM] + [VM] * len(held) + [HB],
        out_specs=(VM,) * len(out),
        out_shape=tuple(out),
        scratch_shapes=[
            pltpu.VMEM((DN_SLOTS, hid, DN_TILE), BF),
            pltpu.SemaphoreType.DMA((DN_SLOTS,)),
        ],
        compiler_params=pltpu.CompilerParams(vmem_limit_bytes=9 * MIB),
        cost_estimate=pl.CostEstimate(
            flops=2 * rows * pieces * cols * hid,
            bytes_accessed=2 * (pieces * cols - n_held * DN_TILE) * hid,
            transcendentals=0,
        ),
        name="down",
    )(me, take, inner, x_own, masks, *held, w_down)


def partner(block, distance):
    devices = range(lax.axis_size("tp"))
    return lax.ppermute(block, "tp", [(i, i ^ distance) for i in devices])


def onward(block, distance):
    tp_count = lax.axis_size("tp")
    sections = lax.axis_size("section")
    route = [
        (s * tp_count + t, (s + 1) % sections * tp_count + (t ^ distance))
        for s in range(sections)
        for t in range(tp_count)
    ]
    return lax.ppermute(block, ("section", "tp"), route)


def beside_exchanged(blocks):
    chips = blocks.shape[0] // 2
    return jnp.concatenate([blocks[:chips], partner(blocks[chips:], 1)], axis=2)


def along_exchanged(both):
    far_first = [partner(both[k], 2 * k) for k in range(both.shape[0] - 1, 0, -1)]
    return [both[0]] + far_first[::-1]


def sorted_arrivals(got):
    got = jnp.stack(got)
    share = got.shape[2] // 2
    return jnp.concatenate([got[:, :, :share], got[:, :, share:]])


def line_of_eight(
    tokens,
    norm_gain,
    gate_weight,
    up_weight,
    gate_mask,
    up_mask,
    down_weight,
    down_mask,
    slot_order,
):
    sections = lax.axis_size("section")
    tp_count = lax.axis_size("tp")
    section_pos = lax.axis_index("section")
    tp_pos = lax.axis_index("tp")
    rows, cols = tokens.shape
    my_blocks = slot_order[0]
    per_device = my_blocks.shape[0]
    chips = tp_count // 2
    me = tp_pos.astype(jnp.int32).reshape(1)

    gate_weight, up_weight, down_weight = (
        pltpu.with_memory_space_constraint(w, pltpu.HBM)
        for w in (gate_weight, up_weight, down_weight)
    )
    numbers = jnp.pad(my_blocks, (0, 128 - per_device)).astype(BF)
    own = jnp.concatenate([tokens, jnp.broadcast_to(numbers[None], (rows, 128))], axis=1)
    send = jnp.zeros((per_device,), jnp.int32)
    gu_masks, dn_masks, norm_gain = spread_masks(
        gate_mask[0].T,
        up_mask[0].T,
        down_mask[0],
        norm_gain,
        gate_weight.shape[2],
        down_weight.shape[2],
    )
    gu_held = [[]] * len(GU_HELD)
    saved = jnp.zeros(tokens.shape, BF)
    for round_pos in range(sections):
        straight = [partner(own, 2 * k) for k in range(chips - 1, 0, -1)]
        beside = partner(own, 1)
        arrivals = gate_up(
            0, me, send, norm_gain, gu_masks, [own[None], beside[None]], [], gu_held[0],
            gate_weight, up_weight,
        )
        if round_pos:
            straight[0], arrivals = lax.optimization_barrier((straight[0], arrivals))
            arrivals = gate_up(
                1, me, send, norm_gain, gu_masks, [straight[0][None]], arrivals, gu_held[1],
                gate_weight, up_weight,
            )
        straight, arrivals = lax.optimization_barrier((straight, arrivals))
        near = jnp.stack(straight)
        far = partner(near, 1)
        part = 2 if round_pos else GU_FIRST_ROUND
        arrivals = gate_up(
            part, me, send, norm_gain, gu_masks,
            [x[None] for x in straight[-len(GU_PARTS[part]) :]], arrivals,
            gu_held[part], gate_weight, up_weight,
        )
        far, arrivals = lax.optimization_barrier((far, arrivals))
        if round_pos == 0:
            send, take = slots(
                me, [own[None], near, beside[None], far], ((0,), (3, 2, 1), (4,), (7, 6, 5)),
                cols, per_device,
            )
        blocks = gate_up(
            3, me, send, norm_gain, gu_masks, [far], arrivals, gu_held[3],
            gate_weight, up_weight,
        )
        both, turn = lax.optimization_barrier((beside_exchanged(blocks), me))
        parts = [part for part, count in enumerate(DN_HELD) if count]
        tiles = hold(
            tuple(DN_PARTS[part] for part in parts),
            tuple(DN_HELD[part] for part in parts),
            turn,
            (down_weight,),
        )
        got, tiles = lax.optimization_barrier((along_exchanged(both), tiles))
        dn_held = [[]] * len(DN_HELD)
        for part, held in zip(parts, tiles):
            dn_held[part] = [held]
        arrived = sorted_arrivals(got)
        passed, mine = down(0, me, take, arrived, own, dn_masks, dn_held[0], down_weight)
        got = partner(passed, 1).astype(F32)
        (kept,) = down(1, me, take, mine, own, dn_masks, dn_held[1], down_weight)
        outward, mine = lax.optimization_barrier(((kept + got).astype(BF), mine))
        nearer = partner(outward, 2)
        kept, passed = down(2, me, take, mine, own, dn_masks, dn_held[2], down_weight)
        nearer, kept, passed = lax.optimization_barrier((nearer, kept, passed))
        sums = kept[2:] + partner(passed, 1).astype(F32) + nearer.astype(F32)
        sums = sums.astype(BF)
        sums, turn = lax.optimization_barrier((sums, me))
        parts = GU_BROUGHT if round_pos else GU_BROUGHT + GU_STAYING
        far_half = onward(sums[1], 4)
        halves = [far_half, onward(sums[0], 0)]
        if round_pos + 1 < sections:
            tiles = held_parts(parts, turn, gate_weight, up_weight)
            halves, tiles = lax.optimization_barrier((halves, tiles))
            for part, held in zip(parts, tiles):
                gu_held[part] = [held]
        own = (halves[0].astype(F32) + halves[1].astype(F32)).astype(BF)
        saved = jnp.where(section_pos == (round_pos + 1) % sections, own, saved)
    return saved[None]


def solution(mesh):
    tp_count = mesh.shape["tp"]
    line_body = line_of_eight if tp_count == 8 else ring_body
    return jax.shard_map(
        line_body,
        mesh=mesh,
        in_specs=(
            P(None, "tp"),
            P("section", None),
            P("section", None, "tp"),
            P("section", None, "tp"),
            P("section", None, "tp"),
            P("section", None, "tp"),
            P("section", "tp", None),
            P("section", "tp", None),
            P("section", "tp"),
        ),
        out_specs=P("section", None, "tp"),
        check_vma=False,
    )
```

profile of v0, /device:TPU:0, one launch (start us, length us, event | category | flops | bytes accessed | tf_op | source)
XLA Modules:
  0.0 288.8 jit_solution(17808216659023775346)
XLA Ops:
  2.1 4.7 %collective-permute-start = (bf16[64,1152]{1,0:T(8,128)(2,1)S(1)}, bf16[64,1152]{1,0:T(8,128)(2,1)S(1)}, u32[]{:S(2)}, u32[]{:S(2)}) collective-permute-start(bf16[64,1152]{1,0:T(8,128)(2,1)S(1)} %get-tuple-element.399.x_ref), channel_id=1, source_target_pairs={{0,6},{1,7},{2,4},{3,5},{4,2},{5,3},{6,0},{7,1},{8,14},{9,15},{10,... | collective-permute-start | bytes 442376 | tf_op jit(solution)/shard_map/ppermute | solution.py:588
  8.9 7.2 %gate_up.15 = (f32[2,64,2048]{2,1,0:T(8,128)S(1)}, f32[64,128]{1,0:T(8,128)S(1)}) custom-call(s32[1]{0:T(128)} %bitcast.me_ref, s32[32]{0:T(128)S(1)} %broadcast_in_dim.61.send_ref, f32[1,8192]{1,0:T(1,128)S(1)} %get-tuple-element.182.gain_ref, f32[2,128,2048]{2,1,0:T(8,128)S(1)} %get-tuple-element.183.masks, ...), custom_call_target="tpu_custom_call" | custom-call | flops 1073741824 | bytes 16777216 | tf_op jit(solution)/shard_map/gate_up/pallas_call | solution.py:458
  16.1 3.8 %collective-permute-done.1 = bf16[64,1152]{1,0:T(8,128)(2,1)S(1)} collective-permute-done((bf16[64,1152]{1,0:T(8,128)(2,1)S(1)}, bf16[64,1152]{1,0:T(8,128)(2,1)S(1)}, u32[]{:S(2)}, u32[]{:S(2)}) %collective-permute-start.1) | collective-permute-done | bytes 147488 | tf_op jit(solution)/shard_map/ppermute | solution.py:588
  20.0 9.6 %gate_up.16 = (f32[2,64,2048]{2,1,0:T(8,128)S(1)}, f32[64,128]{1,0:T(8,128)S(1)}) custom-call(s32[1]{0:T(128)} %bitcast.me_ref, s32[32]{0:T(128)S(1)} %broadcast_in_dim.61.send_ref, f32[1,8192]{1,0:T(1,128)S(1)} %get-tuple-element.182.gain_ref, f32[2,128,2048]{2,1,0:T(8,128)S(1)} %get-tuple-element.183.masks, bf16[1,64,1152]{2,1,0:T(8,128)(2,1)S(1)} %bitcast.104, ...), custom_call_target="tpu_custom_call" | custom-call | flops 1610612736 | bytes 25165824 | tf_op jit(solution)/shard_map/gate_up/pallas_call | solution.py:458
  32.1 10.1 %gate_up.17 = bf16[8,64,256]{2,1,0:T(8,128)(2,1)S(1)} custom-call(s32[1]{0:T(128)} %bitcast.me_ref, s32[32]{0:T(128)S(1)} %get-tuple-element.195.send_ref, f32[1,8192]{1,0:T(1,128)S(1)} %get-tuple-element.182.gain_ref, f32[2,128,2048]{2,1,0:T(8,128)S(1)} %get-tuple-element.183.masks, bf16[3,64,1152]{2,1,0:T(8,128)(2,1)S(1)} %collective-permute-done.4.refs_3_.refs_0_, ...), custom_call_target="tpu_custom_call" | custom-call | flops 1610612736 | bytes 25165824 | tf_op jit(solution)/shard_map/gate_up/pallas_call | solution.py:458
  48.4 6.0 %hold.7 = (bf16[4,2048,512]{2,1,0:T(8,128)(2,1)S(1)}, bf16[4,2048,512]{2,1,0:T(8,128)(2,1)S(1)}) custom-call(s32[1]{0:T(128)} %bitcast.me_ref, bf16[1,2048,8192]{2,1,0:T(8,128)(2,1)} %refs_0_.21), custom_call_target="tpu_custom_call" | custom-call | bytes 16777216 | tf_op jit(solution)/shard_map/hold/pallas_call | solution.py:302
  54.5 3.1 %down.12 = (bf16[2,64,1024]{2,1,0:T(8,128)(2,1)S(1)}, bf16[64,2048]{1,0:T(8,128)(2,1)S(1)}) custom-call(s32[1]{0:T(128)} %bitcast.me_ref, s32[32]{0:T(128)S(1)} %get-tuple-element.194.take_ref, bf16[8,64,256]{2,1,0:T(8,128)(2,1)S(1)} %pad_maximum_fusion.6.inner_ref, bf16[64,1152]{1,0:T(8,128)(2,1)S(1)} %get-tuple-element.399.x_ref, ...), custom_call_target="tpu_custom_call" | custom-call | flops 536870912 | tf_op jit(solution)/shard_map/down/pallas_call | solution.py:567
  60.5 7.6 %down.14 = (f32[4,64,1024]{2,1,0:T(8,128)S(1)}, bf16[2,64,1024]{2,1,0:T(8,128)(2,1)S(1)}) custom-call(s32[1]{0:T(128)} %bitcast.me_ref, s32[32]{0:T(128)S(1)} %get-tuple-element.194.take_ref, bf16[64,2048]{1,0:T(8,128)(2,1)S(1)} %get-tuple-element.212.inner_ref, bf16[64,1152]{1,0:T(8,128)(2,1)S(1)} %get-tuple-element.399.x_ref, ...), custom_call_target="tpu_custom_call" | custom-call | flops 1073741824 | bytes 16777216 | tf_op jit(solution)/shard_map/down/pallas_call | solution.py:567
  75.4 10.8 %hold.8 = (bf16[2,2,512,2048]{3,2,1,0:T(8,128)(2,1)S(1)}, bf16[1,2,512,2048]{3,2,1,0:T(8,128)(2,1)S(1)}, bf16[2,2,512,2048]{3,2,1,0:T(8,128)(2,1)S(1)}, bf16[3,2,512,2048]{3,2,1,0:T(8,128)(2,1)S(1)}) custom-call(s32[1]{0:T(128)} %bitcast.me_ref, bf16[1,8192,2048]{2,1,0:T(8,128)(2,1)} %refs_4_.19, bf16[1,8192,2048]{2,1,0:T(8,128)(2,1)} %refs_5_.19), custom_call_target="tpu_custom_call" | custom-call | bytes 33554432 | tf_op jit(solution)/shard_map/hold/pallas_call | solution.py:302
  90.9 5.1 %gate_up.18 = (f32[2,64,2048]{2,1,0:T(8,128)S(1)}, f32[64,128]{1,0:T(8,128)S(1)}) custom-call(s32[1]{0:T(128)} %bitcast.me_ref, s32[32]{0:T(128)S(1)} %get-tuple-element.195.send_ref, f32[1,8192]{1,0:T(1,128)S(1)} %get-tuple-element.182.gain_ref, f32[2,128,2048]{2,1,0:T(8,128)S(1)} %get-tuple-element.183.masks, bf16[1,64,1024]{2,1,0:T(8,128)(2,1)S(1)} %bitcast.100, ...), custom_call_target="tpu_custom_call" | custom-call | flops 1073741824 | bytes 8388608 | tf_op jit(solution)/shard_map/gate_up/pallas_call | solution.py:458
  96.0 3.7 %gate_up.19 = (f32[2,64,2048]{2,1,0:T(8,128)S(1)}, f32[64,128]{1,0:T(8,128)S(1)}) custom-call(s32[1]{0:T(128)} %bitcast.me_ref, s32[32]{0:T(128)S(1)} %get-tuple-element.195.send_ref, f32[1,8192]{1,0:T(1,128)S(1)} %get-tuple-element.182.gain_ref, f32[2,128,2048]{2,1,0:T(8,128)S(1)} %get-tuple-element.183.masks, bf16[1,64,1024]{2,1,0:T(8,128)(2,1)S(1)} %bitcast.123, ...), custom_call_target="tpu_custom_call" | custom-call | flops 536870912 | bytes 4194304 | tf_op jit(solution)/shard_map/gate_up/pallas_call | solution.py:458
  101.5 5.2 %gate_up.20 = (f32[2,64,2048]{2,1,0:T(8,128)S(1)}, f32[64,128]{1,0:T(8,128)S(1)}) custom-call(s32[1]{0:T(128)} %bitcast.me_ref, s32[32]{0:T(128)S(1)} %get-tuple-element.195.send_ref, f32[1,8192]{1,0:T(1,128)S(1)} %get-tuple-element.182.gain_ref, f32[2,128,2048]{2,1,0:T(8,128)S(1)} %get-tuple-element.183.masks, bf16[1,64,1024]{2,1,0:T(8,128)(2,1)S(1)} %bitcast.112, ...), custom_call_target="tpu_custom_call" | custom-call | flops 1073741824 | bytes 8388608 | tf_op jit(solution)/shard_map/gate_up/pallas_call | solution.py:458
  106.6 7.4 %gate_up.21 = bf16[8,64,256]{2,1,0:T(8,128)(2,1)S(1)} custom-call(s32[1]{0:T(128)} %bitcast.me_ref, s32[32]{0:T(128)S(1)} %get-tuple-element.195.send_ref, f32[1,8192]{1,0:T(1,128)S(1)} %get-tuple-element.182.gain_ref, f32[2,128,2048]{2,1,0:T(8,128)S(1)} %get-tuple-element.183.masks, bf16[3,64,1024]{2,1,0:T(8,128)(2,1)S(1)} %collective-permute-done.18.refs_0_, ...), custom_call_target="tpu_custom_call" | custom-call | flops 1610612736 | bytes 12582912 | tf_op jit(solution)/shard_map/gate_up/pallas_call | solution.py:458
  120.1 6.0 %hold.9 = (bf16[4,2048,512]{2,1,0:T(8,128)(2,1)S(1)}, bf16[4,2048,512]{2,1,0:T(8,128)(2,1)S(1)}) custom-call(s32[1]{0:T(128)} %bitcast.me_ref, bf16[1,2048,8192]{2,1,0:T(8,128)(2,1)} %refs_0_.21), custom_call_target="tpu_custom_call" | custom-call | bytes 16777216 | tf_op jit(solution)/shard_map/hold/pallas_call | solution.py:302
  126.3 3.1 %down.15 = (bf16[2,64,1024]{2,1,0:T(8,128)(2,1)S(1)}, bf16[64,2048]{1,0:T(8,128)(2,1)S(1)}) custom-call(s32[1]{0:T(128)} %bitcast.me_ref, s32[32]{0:T(128)S(1)} %get-tuple-element.194.take_ref, bf16[8,64,256]{2,1,0:T(8,128)(2,1)S(1)} %pad_maximum_fusion.9.inner_ref, bf16[64,1024]{1,0:T(8,128)(2,1)S(1)} %add_convert_fusion.11.x_ref, ...), custom_call_target="tpu_custom_call" | custom-call | flops 536870912 | tf_op jit(solution)/shard_map/down/pallas_call | solution.py:567
  133.3 7.6 %down.17 = (f32[4,64,1024]{2,1,0:T(8,128)S(1)}, bf16[2,64,1024]{2,1,0:T(8,128)(2,1)S(1)}) custom-call(s32[1]{0:T(128)} %bitcast.me_ref, s32[32]{0:T(128)S(1)} %get-tuple-element.194.take_ref, bf16[64,2048]{1,0:T(8,128)(2,1)S(1)} %get-tuple-element.260.inner_ref, bf16[64,1024]{1,0:T(8,128)(2,1)S(1)} %add_convert_fusion.11.x_ref, ...), custom_call_target="tpu_custom_call" | custom-call | flops 1073741824 | bytes 16777216 | tf_op jit(solution)/shard_map/down/pallas_call | solution.py:567
  145.1 7.1 %hold.10 = (bf16[2,2,512,2048]{3,2,1,0:T(8,128)(2,1)S(1)}, bf16[1,2,512,2048]{3,2,1,0:T(8,128)(2,1)S(1)}, bf16[2,2,512,2048]{3,2,1,0:T(8,128)(2,1)S(1)}) custom-call(s32[1]{0:T(128)} %bitcast.me_ref, bf16[1,8192,2048]{2,1,0:T(8,128)(2,1)} %refs_4_.19, bf16[1,8192,2048]{2,1,0:T(8,128)(2,1)} %refs_5_.19), custom_call_target="tpu_custom_call" | custom-call | bytes 20971520 | tf_op jit(solution)/shard_map/hold/pallas_call | solution.py:302
  158.5 5.1 %gate_up.22 = (f32[2,64,2048]{2,1,0:T(8,128)S(1)}, f32[64,128]{1,0:T(8,128)S(1)}) custom-call(s32[1]{0:T(128)} %bitcast.me_ref, s32[32]{0:T(128)S(1)} %get-tuple-element.195.send_ref, f32[1,8192]{1,0:T(1,128)S(1)} %get-tuple-element.182.gain_ref, f32[2,128,2048]{2,1,0:T(8,128)S(1)} %get-tuple-element.183.masks, bf16[1,64,1024]{2,1,0:T(8,128)(2,1)S(1)} %bitcast.101, ...), custom_call_target="tpu_custom_call" | custom-call | flops 1073741824 | bytes 8388608 | tf_op jit(solution)/shard_map/gate_up/pallas_call | solution.py:458
  163.6 3.7 %gate_up.23 = (f32[2,64,2048]{2,1,0:T(8,128)S(1)}, f32[64,128]{1,0:T(8,128)S(1)}) custom-call(s32[1]{0:T(128)} %bitcast.me_ref, s32[32]{0:T(128)S(1)} %get-tuple-element.195.send_ref, f32[1,8192]{1,0:T(1,128)S(1)} %get-tuple-element.182.gain_ref, f32[2,128,2048]{2,1,0:T(8,128)S(1)} %get-tuple-element.183.masks, bf16[1,64,1024]{2,1,0:T(8,128)(2,1)S(1)} %bitcast.125, ...), custom_call_target="tpu_custom_call" | custom-call | flops 536870912 | bytes 4194304 | tf_op jit(solution)/shard_map/gate_up/pallas_call | solution.py:458
  168.8 5.2 %gate_up.24 = (f32[2,64,2048]{2,1,0:T(8,128)S(1)}, f32[64,128]{1,0:T(8,128)S(1)}) custom-call(s32[1]{0:T(128)} %bitcast.me_ref, s32[32]{0:T(128)S(1)} %get-tuple-element.195.send_ref, f32[1,8192]{1,0:T(1,128)S(1)} %get-tuple-element.182.gain_ref, f32[2,128,2048]{2,1,0:T(8,128)S(1)} %get-tuple-element.183.masks, bf16[1,64,1024]{2,1,0:T(8,128)(2,1)S(1)} %bitcast.114, ...), custom_call_target="tpu_custom_call" | custom-call | flops 1073741824 | bytes 8388608 | tf_op jit(solution)/shard_map/gate_up/pallas_call | solution.py:458
  173.9 7.4 %gate_up.25 = bf16[8,64,256]{2,1,0:T(8,128)(2,1)S(1)} custom-call(s32[1]{0:T(128)} %bitcast.me_ref, s32[32]{0:T(128)S(1)} %get-tuple-element.195.send_ref, f32[1,8192]{1,0:T(1,128)S(1)} %get-tuple-element.182.gain_ref, f32[2,128,2048]{2,1,0:T(8,128)S(1)} %get-tuple-element.183.masks, bf16[3,64,1024]{2,1,0:T(8,128)(2,1)S(1)} %collective-permute-done.32.refs_0_, ...), custom_call_target="tpu_custom_call" | custom-call | flops 1610612736 | bytes 12582912 | tf_op jit(solution)/shard_map/gate_up/pallas_call | solution.py:458
  187.4 6.0 %hold.11 = (bf16[4,2048,512]{2,1,0:T(8,128)(2,1)S(1)}, bf16[4,2048,512]{2,1,0:T(8,128)(2,1)S(1)}) custom-call(s32[1]{0:T(128)} %bitcast.me_ref, bf16[1,2048,8192]{2,1,0:T(8,128)(2,1)} %refs_0_.21), custom_call_target="tpu_custom_call" | custom-call | bytes 16777216 | tf_op jit(solution)/shard_map/hold/pallas_call | solution.py:302
  193.6 3.1 %down.18 = (bf16[2,64,1024]{2,1,0:T(8,128)(2,1)S(1)}, bf16[64,2048]{1,0:T(8,128)(2,1)S(1)}) custom-call(s32[1]{0:T(128)} %bitcast.me_ref, s32[32]{0:T(128)S(1)} %get-tuple-element.194.take_ref, bf16[8,64,256]{2,1,0:T(8,128)(2,1)S(1)} %pad_maximum_fusion.12.inner_ref, bf16[64,1024]{1,0:T(8,128)(2,1)S(1)} %add_convert_fusion.10.x_ref, ...), custom_call_target="tpu_custom_call" | custom-call | flops 536870912 | tf_op jit(solution)/shard_map/down/pallas_call | solution.py:567
  200.6 7.6 %down.20 = (f32[4,64,1024]{2,1,0:T(8,128)S(1)}, bf16[2,64,1024]{2,1,0:T(8,128)(2,1)S(1)}) custom-call(s32[1]{0:T(128)} %bitcast.me_ref, s32[32]{0:T(128)S(1)} %get-tuple-element.194.take_ref, bf16[64,2048]{1,0:T(8,128)(2,1)S(1)} %get-tuple-element.306.inner_ref, bf16[64,1024]{1,0:T(8,128)(2,1)S(1)} %add_convert_fusion.10.x_ref, ...), custom_call_target="tpu_custom_call" | custom-call | flops 1073741824 | bytes 16777216 | tf_op jit(solution)/shard_map/down/pallas_call | solution.py:567
  213.1 7.1 %hold.12 = (bf16[2,2,512,2048]{3,2,1,0:T(8,128)(2,1)S(1)}, bf16[1,2,512,2048]{3,2,1,0:T(8,128)(2,1)S(1)}, bf16[2,2,512,2048]{3,2,1,0:T(8,128)(2,1)S(1)}) custom-call(s32[1]{0:T(128)} %bitcast.me_ref, bf16[1,8192,2048]{2,1,0:T(8,128)(2,1)} %refs_4_.19, bf16[1,8192,2048]{2,1,0:T(8,128)(2,1)} %refs_5_.19), custom_call_target="tpu_custom_call" | custom-call | bytes 20971520 | tf_op jit(solution)/shard_map/hold/pallas_call | solution.py:302
  225.8 5.1 %gate_up.26 = (f32[2,64,2048]{2,1,0:T(8,128)S(1)}, f32[64,128]{1,0:T(8,128)S(1)}) custom-call(s32[1]{0:T(128)} %bitcast.me_ref, s32[32]{0:T(128)S(1)} %get-tuple-element.195.send_ref, f32[1,8192]{1,0:T(1,128)S(1)} %get-tuple-element.182.gain_ref, f32[2,128,2048]{2,1,0:T(8,128)S(1)} %get-tuple-element.183.masks, bf16[1,64,1024]{2,1,0:T(8,128)(2,1)S(1)} %bitcast.102, ...), custom_call_target="tpu_custom_call" | custom-call | flops 1073741824 | bytes 8388608 | tf_op jit(solution)/shard_map/gate_up/pallas_call | solution.py:458
  230.9 3.7 %gate_up.27 = (f32[2,64,2048]{2,1,0:T(8,128)S(1)}, f32[64,128]{1,0:T(8,128)S(1)}) custom-call(s32[1]{0:T(128)} %bitcast.me_ref, s32[32]{0:T(128)S(1)} %get-tuple-element.195.send_ref, f32[1,8192]{1,0:T(1,128)S(1)} %get-tuple-element.182.gain_ref, f32[2,128,2048]{2,1,0:T(8,128)S(1)} %get-tuple-element.183.masks, bf16[1,64,1024]{2,1,0:T(8,128)(2,1)S(1)} %bitcast.127, ...), custom_call_target="tpu_custom_call" | custom-call | flops 536870912 | bytes 4194304 | tf_op jit(solution)/shard_map/gate_up/pallas_call | solution.py:458
  235.6 5.2 %gate_up.28 = (f32[2,64,2048]{2,1,0:T(8,128)S(1)}, f32[64,128]{1,0:T(8,128)S(1)}) custom-call(s32[1]{0:T(128)} %bitcast.me_ref, s32[32]{0:T(128)S(1)} %get-tuple-element.195.send_ref, f32[1,8192]{1,0:T(1,128)S(1)} %get-tuple-element.182.gain_ref, f32[2,128,2048]{2,1,0:T(8,128)S(1)} %get-tuple-element.183.masks, bf16[1,64,1024]{2,1,0:T(8,128)(2,1)S(1)} %bitcast.116, ...), custom_call_target="tpu_custom_call" | custom-call | flops 1073741824 | bytes 8388608 | tf_op jit(solution)/shard_map/gate_up/pallas_call | solution.py:458
  240.8 7.4 %gate_up.29 = bf16[8,64,256]{2,1,0:T(8,128)(2,1)S(1)} custom-call(s32[1]{0:T(128)} %bitcast.me_ref, s32[32]{0:T(128)S(1)} %get-tuple-element.195.send_ref, f32[1,8192]{1,0:T(1,128)S(1)} %get-tuple-element.182.gain_ref, f32[2,128,2048]{2,1,0:T(8,128)S(1)} %get-tuple-element.183.masks, bf16[3,64,1024]{2,1,0:T(8,128)(2,1)S(1)} %collective-permute-done.46.refs_0_, ...), custom_call_target="tpu_custom_call" | custom-call | flops 1610612736 | bytes 12582912 | tf_op jit(solution)/shard_map/gate_up/pallas_call | solution.py:458
  254.3 6.0 %hold.13 = (bf16[4,2048,512]{2,1,0:T(8,128)(2,1)S(1)}, bf16[4,2048,512]{2,1,0:T(8,128)(2,1)S(1)}) custom-call(s32[1]{0:T(128)} %bitcast.me_ref, bf16[1,2048,8192]{2,1,0:T(8,128)(2,1)} %refs_0_.21), custom_call_target="tpu_custom_call" | custom-call | bytes 16777216 | tf_op jit(solution)/shard_map/hold/pallas_call | solution.py:302
  267.5 7.6 %down.23 = (f32[4,64,1024]{2,1,0:T(8,128)S(1)}, bf16[2,64,1024]{2,1,0:T(8,128)(2,1)S(1)}) custom-call(s32[1]{0:T(128)} %bitcast.me_ref, s32[32]{0:T(128)S(1)} %get-tuple-element.194.take_ref, bf16[64,2048]{1,0:T(8,128)(2,1)S(1)} %get-tuple-element.352.inner_ref, bf16[64,1024]{1,0:T(8,128)(2,1)S(1)} %add_convert_fusion.9.x_ref, ...), custom_call_target="tpu_custom_call" | custom-call | flops 1073741824 | bytes 16777216 | tf_op jit(solution)/shard_map/down/pallas_call | solution.py:567
  280.5 7.5 %collective-permute-done.54 = bf16[64,1024]{1,0:T(8,128)(2,1)S(1)} collective-permute-done((bf16[64,1024]{1,0:T(8,128)(2,1)S(1)}, bf16[64,1024]{1,0:T(8,128)(2,1)S(1)}, u32[]{:S(2)}, u32[]{:S(2)}) %collective-permute-start.54) | collective-permute-done | bytes 131104 | tf_op jit(solution)/shard_map/ppermute | solution.py:599
  (172 shorter events, 91.8 us)
Async XLA Ops:
  2.1 14.0 %collective-permute-start = (bf16[64,1152]{1,0:T(8,128)(2,1)S(1)}, bf16[64,1152]{1,0:T(8,128)(2,1)S(1)}, u32[]{:S(2)}, u32[]{:S(2)}) collective-permute-start(bf16[64,1152]{1,0:T(8,128)(2,1)S(1)} %get-tuple-element.399.x_ref), channel_id=1, source_target_pairs={{0,6},{1,7},{2,4},{3,5},{4,2},{5,3},{6,0},{7,1},{8,14},{9,15},{10,... | collective-permute-start | bytes 442376 | tf_op jit(solution)/shard_map/ppermute | solution.py:588
  6.8 13.1 %collective-permute-start.1 = (bf16[64,1152]{1,0:T(8,128)(2,1)S(1)}, bf16[64,1152]{1,0:T(8,128)(2,1)S(1)}, u32[]{:S(2)}, u32[]{:S(2)}) collective-permute-start(bf16[64,1152]{1,0:T(8,128)(2,1)S(1)} %get-tuple-element.399.x_ref), channel_id=1, source_target_pairs={{0,4},{1,5},{2,6},{3,7},{4,0},{5,1},{6,2},{7,3},{8,12},{9,13},{10,... | collective-permute-start | bytes 442376 | tf_op jit(solution)/shard_map/ppermute | solution.py:588
  6.8 13.1 %collective-permute-start.2 = (bf16[64,1152]{1,0:T(8,128)(2,1)S(1)}, bf16[64,1152]{1,0:T(8,128)(2,1)S(1)}, u32[]{:S(2)}, u32[]{:S(2)}) collective-permute-start(bf16[64,1152]{1,0:T(8,128)(2,1)S(1)} %get-tuple-element.399.x_ref), channel_id=1, source_target_pairs={{0,2},{1,3},{2,0},{3,1},{4,6},{5,7},{6,4},{7,5},{8,10},{9,11},{10,... | collective-permute-start | bytes 442376 | tf_op jit(solution)/shard_map/ppermute | solution.py:588
  20.0 9.7 %collective-permute-start.4 = (bf16[3,64,1152]{2,1,0:T(8,128)(2,1)S(1)}, bf16[3,64,1152]{2,1,0:T(8,128)(2,1)S(1)}, u32[]{:S(2)}, u32[]{:S(2)}) collective-permute-start(bf16[3,64,1152]{2,1,0:T(8,128)(2,1)S(1)} %pad_maximum_fusion.refs_1_), channel_id=1, source_target_pairs={{0,1},{1,0},{2,3},{3,2},{4,5},{5,4},{6,7},{7,6},{8,9},{9,8},{10,11... | collective-permute-start | bytes 1327112 | tf_op jit(solution)/shard_map/ppermute | solution.py:588
  43.9 10.5 %collective-permute-start.6 = (bf16[64,512]{1,0:T(8,128)(2,1)S(1)}, bf16[64,512]{1,0:T(8,128)(2,1)S(1)}, u32[]{:S(2)}, u32[]{:S(2)}) collective-permute-start(bf16[64,512]{1,0:T(8,128)(2,1)S(1)} %get-tuple-element.395), channel_id=1, source_target_pairs={{0,2},{1,3},{2,0},{3,1},{4,6},{5,7},{6,4},{7,5},{8,10},{9,11},{10,... | collective-permute-start | bytes 196616 | tf_op jit(solution)/shard_map/ppermute | solution.py:588
  44.0 10.4 %collective-permute-start.7 = (bf16[64,512]{1,0:T(8,128)(2,1)S(1)}, bf16[64,512]{1,0:T(8,128)(2,1)S(1)}, u32[]{:S(2)}, u32[]{:S(2)}) collective-permute-start(bf16[64,512]{1,0:T(8,128)(2,1)S(1)} %get-tuple-element.394), channel_id=1, source_target_pairs={{0,4},{1,5},{2,6},{3,7},{4,0},{5,1},{6,2},{7,3},{8,12},{9,13},{10,... | collective-permute-start | bytes 196616 | tf_op jit(solution)/shard_map/ppermute | solution.py:588
  60.4 8.8 %collective-permute-start.10 = (bf16[2,64,1024]{2,1,0:T(8,128)(2,1)S(1)}, bf16[2,64,1024]{2,1,0:T(8,128)(2,1)S(1)}, u32[]{:S(2)}, u32[]{:S(2)}) collective-permute-start(bf16[2,64,1024]{2,1,0:T(8,128)(2,1)S(1)} %add_convert_fusion.7), channel_id=1, source_target_pairs={{0,2},{1,3},{2,0},{3,1},{4,6},{5,7},{6,4},{7,5},{8,10},{9,11},{10,... | collective-permute-start | bytes 786440 | tf_op jit(solution)/shard_map/ppermute | solution.py:588
  70.9 15.4 %collective-permute-start.12 = (bf16[64,1024]{1,0:T(8,128)(2,1)S(1)}, bf16[64,1024]{1,0:T(8,128)(2,1)S(1)}, u32[]{:S(2)}, u32[]{:S(2)}) collective-permute-start(bf16[64,1024]{1,0:T(8,128)(2,1)S(1)} %get-tuple-element.390), channel_id=1, source_target_pairs={{0,12},{1,13},{2,14},{3,15},{4,8},{5,9},{6,10},{7,11},{8,20},{9,21... | collective-permute-start | bytes 393224 | tf_op jit(solution)/shard_map/ppermute | solution.py:599
  73.9 12.3 %collective-permute-start.13 = (bf16[64,1024]{1,0:T(8,128)(2,1)S(1)}, bf16[64,1024]{1,0:T(8,128)(2,1)S(1)}, u32[]{:S(2)}, u32[]{:S(2)}) collective-permute-start(bf16[64,1024]{1,0:T(8,128)(2,1)S(1)} %get-tuple-element.389), channel_id=1, source_target_pairs={{0,8},{1,9},{2,10},{3,11},{4,12},{5,13},{6,14},{7,15},{8,16},{9,17... | collective-permute-start | bytes 393224 | tf_op jit(solution)/shard_map/ppermute | solution.py:599
  86.4 9.6 %collective-permute-start.14 = (bf16[64,1024]{1,0:T(8,128)(2,1)S(1)}, bf16[64,1024]{1,0:T(8,128)(2,1)S(1)}, u32[]{:S(2)}, u32[]{:S(2)}) collective-permute-start(bf16[64,1024]{1,0:T(8,128)(2,1)S(1)} %add_convert_fusion.11.x_ref), channel_id=1, source_target_pairs={{0,6},{1,7},{2,4},{3,5},{4,2},{5,3},{6,0},{7,1},{8,14},{9,15},{10,... | collective-permute-start | bytes 393224 | tf_op jit(solution)/shard_map/ppermute | solution.py:588
  88.0 13.3 %collective-permute-start.16 = (bf16[64,1024]{1,0:T(8,128)(2,1)S(1)}, bf16[64,1024]{1,0:T(8,128)(2,1)S(1)}, u32[]{:S(2)}, u32[]{:S(2)}) collective-permute-start(bf16[64,1024]{1,0:T(8,128)(2,1)S(1)} %add_convert_fusion.11.x_ref), channel_id=1, source_target_pairs={{0,4},{1,5},{2,6},{3,7},{4,0},{5,1},{6,2},{7,3},{8,12},{9,13},{10,... | collective-permute-start | bytes 393224 | tf_op jit(solution)/shard_map/ppermute | solution.py:588
  89.1 12.3 %collective-permute-start.17 = (bf16[64,1024]{1,0:T(8,128)(2,1)S(1)}, bf16[64,1024]{1,0:T(8,128)(2,1)S(1)}, u32[]{:S(2)}, u32[]{:S(2)}) collective-permute-start(bf16[64,1024]{1,0:T(8,128)(2,1)S(1)} %add_convert_fusion.11.x_ref), channel_id=1, source_target_pairs={{0,2},{1,3},{2,0},{3,1},{4,6},{5,7},{6,4},{7,5},{8,10},{9,11},{10,... | collective-permute-start | bytes 393224 | tf_op jit(solution)/shard_map/ppermute | solution.py:588
  115.7 10.5 %collective-permute-start.20 = (bf16[64,512]{1,0:T(8,128)(2,1)S(1)}, bf16[64,512]{1,0:T(8,128)(2,1)S(1)}, u32[]{:S(2)}, u32[]{:S(2)}) collective-permute-start(bf16[64,512]{1,0:T(8,128)(2,1)S(1)} %get-tuple-element.385), channel_id=1, source_target_pairs={{0,2},{1,3},{2,0},{3,1},{4,6},{5,7},{6,4},{7,5},{8,10},{9,11},{10,... | collective-permute-start | bytes 196616 | tf_op jit(solution)/shard_map/ppermute | solution.py:588
  117.6 8.6 %collective-permute-start.22 = (bf16[64,512]{1,0:T(8,128)(2,1)S(1)}, bf16[64,512]{1,0:T(8,128)(2,1)S(1)}, u32[]{:S(2)}, u32[]{:S(2)}) collective-permute-start(bf16[64,512]{1,0:T(8,128)(2,1)S(1)} %get-tuple-element.383), channel_id=1, source_target_pairs={{0,6},{1,7},{2,4},{3,5},{4,2},{5,3},{6,0},{7,1},{8,14},{9,15},{10,... | collective-permute-start | bytes 196616 | tf_op jit(solution)/shard_map/ppermute | solution.py:588
  132.2 8.8 %collective-permute-start.24 = (bf16[2,64,1024]{2,1,0:T(8,128)(2,1)S(1)}, bf16[2,64,1024]{2,1,0:T(8,128)(2,1)S(1)}, u32[]{:S(2)}, u32[]{:S(2)}) collective-permute-start(bf16[2,64,1024]{2,1,0:T(8,128)(2,1)S(1)} %add_convert_fusion.5), channel_id=1, source_target_pairs={{0,2},{1,3},{2,0},{3,1},{4,6},{5,7},{6,4},{7,5},{8,10},{9,11},{10,... | collective-permute-start | bytes 786440 | tf_op jit(solution)/shard_map/ppermute | solution.py:588
  142.7 11.2 %collective-permute-start.26 = (bf16[64,1024]{1,0:T(8,128)(2,1)S(1)}, bf16[64,1024]{1,0:T(8,128)(2,1)S(1)}, u32[]{:S(2)}, u32[]{:S(2)}) collective-permute-start(bf16[64,1024]{1,0:T(8,128)(2,1)S(1)} %get-tuple-element.380), channel_id=1, source_target_pairs={{0,12},{1,13},{2,14},{3,15},{4,8},{5,9},{6,10},{7,11},{8,20},{9,21... | collective-permute-start | bytes 393224 | tf_op jit(solution)/shard_map/ppermute | solution.py:599
  144.6 9.2 %collective-permute-start.27 = (bf16[64,1024]{1,0:T(8,128)(2,1)S(1)}, bf16[64,1024]{1,0:T(8,128)(2,1)S(1)}, u32[]{:S(2)}, u32[]{:S(2)}) collective-permute-start(bf16[64,1024]{1,0:T(8,128)(2,1)S(1)} %get-tuple-element.379), channel_id=1, source_target_pairs={{0,8},{1,9},{2,10},{3,11},{4,12},{5,13},{6,14},{7,15},{8,16},{9,17... | collective-permute-start | bytes 393224 | tf_op jit(solution)/shard_map/ppermute | solution.py:599
  154.0 9.6 %collective-permute-start.28 = (bf16[64,1024]{1,0:T(8,128)(2,1)S(1)}, bf16[64,1024]{1,0:T(8,128)(2,1)S(1)}, u32[]{:S(2)}, u32[]{:S(2)}) collective-permute-start(bf16[64,1024]{1,0:T(8,128)(2,1)S(1)} %add_convert_fusion.10.x_ref), channel_id=1, source_target_pairs={{0,6},{1,7},{2,4},{3,5},{4,2},{5,3},{6,0},{7,1},{8,14},{9,15},{10,... | collective-permute-start | bytes 393224 | tf_op jit(solution)/shard_map/ppermute | solution.py:588
  155.8 12.8 %collective-permute-start.30 = (bf16[64,1024]{1,0:T(8,128)(2,1)S(1)}, bf16[64,1024]{1,0:T(8,128)(2,1)S(1)}, u32[]{:S(2)}, u32[]{:S(2)}) collective-permute-start(bf16[64,1024]{1,0:T(8,128)(2,1)S(1)} %add_convert_fusion.10.x_ref), channel_id=1, source_target_pairs={{0,4},{1,5},{2,6},{3,7},{4,0},{5,1},{6,2},{7,3},{8,12},{9,13},{10,... | collective-permute-start | bytes 393224 | tf_op jit(solution)/shard_map/ppermute | solution.py:588
  156.4 12.3 %collective-permute-start.31 = (bf16[64,1024]{1,0:T(8,128)(2,1)S(1)}, bf16[64,1024]{1,0:T(8,128)(2,1)S(1)}, u32[]{:S(2)}, u32[]{:S(2)}) collective-permute-start(bf16[64,1024]{1,0:T(8,128)(2,1)S(1)} %add_convert_fusion.10.x_ref), channel_id=1, source_target_pairs={{0,2},{1,3},{2,0},{3,1},{4,6},{5,7},{6,4},{7,5},{8,10},{9,11},{10,... | collective-permute-start | bytes 393224 | tf_op jit(solution)/shard_map/ppermute | solution.py:588
  183.0 10.5 %collective-permute-start.34 = (bf16[64,512]{1,0:T(8,128)(2,1)S(1)}, bf16[64,512]{1,0:T(8,128)(2,1)S(1)}, u32[]{:S(2)}, u32[]{:S(2)}) collective-permute-start(bf16[64,512]{1,0:T(8,128)(2,1)S(1)} %get-tuple-element.375), channel_id=1, source_target_pairs={{0,2},{1,3},{2,0},{3,1},{4,6},{5,7},{6,4},{7,5},{8,10},{9,11},{10,... | collective-permute-start | bytes 196616 | tf_op jit(solution)/shard_map/ppermute | solution.py:588
  199.5 8.8 %collective-permute-start.38 = (bf16[2,64,1024]{2,1,0:T(8,128)(2,1)S(1)}, bf16[2,64,1024]{2,1,0:T(8,128)(2,1)S(1)}, u32[]{:S(2)}, u32[]{:S(2)}) collective-permute-start(bf16[2,64,1024]{2,1,0:T(8,128)(2,1)S(1)} %add_convert_fusion.3), channel_id=1, source_target_pairs={{0,2},{1,3},{2,0},{3,1},{4,6},{5,7},{6,4},{7,5},{8,10},{9,11},{10,... | collective-permute-start | bytes 786440 | tf_op jit(solution)/shard_map/ppermute | solution.py:588
  210.0 11.2 %collective-permute-start.40 = (bf16[64,1024]{1,0:T(8,128)(2,1)S(1)}, bf16[64,1024]{1,0:T(8,128)(2,1)S(1)}, u32[]{:S(2)}, u32[]{:S(2)}) collective-permute-start(bf16[64,1024]{1,0:T(8,128)(2,1)S(1)} %get-tuple-element.370), channel_id=1, source_target_pairs={{0,12},{1,13},{2,14},{3,15},{4,8},{5,9},{6,10},{7,11},{8,20},{9,21... | collective-permute-start | bytes 393224 | tf_op jit(solution)/shard_map/ppermute | solution.py:599
  211.5 9.7 %collective-permute-start.41 = (bf16[64,1024]{1,0:T(8,128)(2,1)S(1)}, bf16[64,1024]{1,0:T(8,128)(2,1)S(1)}, u32[]{:S(2)}, u32[]{:S(2)}) collective-permute-start(bf16[64,1024]{1,0:T(8,128)(2,1)S(1)} %get-tuple-element.369), channel_id=1, source_target_pairs={{0,8},{1,9},{2,10},{3,11},{4,12},{5,13},{6,14},{7,15},{8,16},{9,17... | collective-permute-start | bytes 393224 | tf_op jit(solution)/shard_map/ppermute | solution.py:599
  221.3 9.6 %collective-permute-start.42 = (bf16[64,1024]{1,0:T(8,128)(2,1)S(1)}, bf16[64,1024]{1,0:T(8,128)(2,1)S(1)}, u32[]{:S(2)}, u32[]{:S(2)}) collective-permute-start(bf16[64,1024]{1,0:T(8,128)(2,1)S(1)} %add_convert_fusion.9.x_ref), channel_id=1, source_target_pairs={{0,6},{1,7},{2,4},{3,5},{4,2},{5,3},{6,0},{7,1},{8,14},{9,15},{10,... | collective-permute-start | bytes 393224 | tf_op jit(solution)/shard_map/ppermute | solution.py:588
  223.1 12.4 %collective-permute-start.44 = (bf16[64,1024]{1,0:T(8,128)(2,1)S(1)}, bf16[64,1024]{1,0:T(8,128)(2,1)S(1)}, u32[]{:S(2)}, u32[]{:S(2)}) collective-permute-start(bf16[64,1024]{1,0:T(8,128)(2,1)S(1)} %add_convert_fusion.9.x_ref), channel_id=1, source_target_pairs={{0,4},{1,5},{2,6},{3,7},{4,0},{5,1},{6,2},{7,3},{8,12},{9,13},{10,... | collective-permute-start | bytes 393224 | tf_op jit(solution)/shard_map/ppermute | solution.py:588
  223.2 12.3 %collective-permute-start.45 = (bf16[64,1024]{1,0:T(8,128)(2,1)S(1)}, bf16[64,1024]{1,0:T(8,128)(2,1)S(1)}, u32[]{:S(2)}, u32[]{:S(2)}) collective-permute-start(bf16[64,1024]{1,0:T(8,128)(2,1)S(1)} %add_convert_fusion.9.x_ref), channel_id=1, source_target_pairs={{0,2},{1,3},{2,0},{3,1},{4,6},{5,7},{6,4},{7,5},{8,10},{9,11},{10,... | collective-permute-start | bytes 393224 | tf_op jit(solution)/shard_map/ppermute | solution.py:588
  249.8 10.5 %collective-permute-start.48 = (bf16[64,512]{1,0:T(8,128)(2,1)S(1)}, bf16[64,512]{1,0:T(8,128)(2,1)S(1)}, u32[]{:S(2)}, u32[]{:S(2)}) collective-permute-start(bf16[64,512]{1,0:T(8,128)(2,1)S(1)} %get-tuple-element.365), channel_id=1, source_target_pairs={{0,2},{1,3},{2,0},{3,1},{4,6},{5,7},{6,4},{7,5},{8,10},{9,11},{10,... | collective-permute-start | bytes 196616 | tf_op jit(solution)/shard_map/ppermute | solution.py:588
  251.7 8.6 %collective-permute-start.49 = (bf16[64,512]{1,0:T(8,128)(2,1)S(1)}, bf16[64,512]{1,0:T(8,128)(2,1)S(1)}, u32[]{:S(2)}, u32[]{:S(2)}) collective-permute-start(bf16[64,512]{1,0:T(8,128)(2,1)S(1)} %get-tuple-element.364), channel_id=1, source_target_pairs={{0,4},{1,5},{2,6},{3,7},{4,0},{5,1},{6,2},{7,3},{8,12},{9,13},{10,... | collective-permute-start | bytes 196616 | tf_op jit(solution)/shard_map/ppermute | solution.py:588
  266.3 8.8 %collective-permute-start.52 = (bf16[2,64,1024]{2,1,0:T(8,128)(2,1)S(1)}, bf16[2,64,1024]{2,1,0:T(8,128)(2,1)S(1)}, u32[]{:S(2)}, u32[]{:S(2)}) collective-permute-start(bf16[2,64,1024]{2,1,0:T(8,128)(2,1)S(1)} %add_convert_fusion.1), channel_id=1, source_target_pairs={{0,2},{1,3},{2,0},{3,1},{4,6},{5,7},{6,4},{7,5},{8,10},{9,11},{10,... | collective-permute-start | bytes 786440 | tf_op jit(solution)/shard_map/ppermute | solution.py:588
  276.9 11.2 %collective-permute-start.54 = (bf16[64,1024]{1,0:T(8,128)(2,1)S(1)}, bf16[64,1024]{1,0:T(8,128)(2,1)S(1)}, u32[]{:S(2)}, u32[]{:S(2)}) collective-permute-start(bf16[64,1024]{1,0:T(8,128)(2,1)S(1)} %get-tuple-element.359), channel_id=1, source_target_pairs={{0,12},{1,13},{2,14},{3,15},{4,8},{5,9},{6,10},{7,11},{8,20},{9,21... | collective-permute-start | bytes 393224 | tf_op jit(solution)/shard_map/ppermute | solution.py:599
  278.7 9.4 %collective-permute-start.55 = (bf16[64,1024]{1,0:T(8,128)(2,1)S(1)}, bf16[64,1024]{1,0:T(8,128)(2,1)S(1)}, u32[]{:S(2)}, u32[]{:S(2)}) collective-permute-start(bf16[64,1024]{1,0:T(8,128)(2,1)S(1)} %get-tuple-element.360), channel_id=1, source_target_pairs={{0,8},{1,9},{2,10},{3,11},{4,12},{5,13},{6,14},{7,15},{8,16},{9,17... | collective-permute-start | bytes 393224 | tf_op jit(solution)/shard_map/ppermute | solution.py:599
  (28 other events, 238.3 us)
where the time goes:
time: 289 us
  Pallas kernels  197 us (68%)
  starting transfers between devices  58 us (20%)
  waiting for transfers between devices  28.4 us (10%)
  other arithmetic  3.57 us (1%)
    pallas_call x15, Pallas kernels, gate_up(): pl.pallas_call(functools.partial(gate_up_kernel, part, len(xs), len(befor...  90.9 us
    pallas_call x12, Pallas kernels, down(): pl.pallas_call(functools.partial(down_kernel, part, n_held), in_specs=[SM...  53.4 us
    pallas_call x7, Pallas kernels, hold(): pl.pallas_call(functools.partial(hold_kernel, parts), in_specs=[SM] + [HB...  49.2 us
    ppermute x48, starting transfers between devices, partner(): return lax.ppermute(block, 'tp', [(i, i ^ distance) for i in devices])  44.3 us
    ppermute x48, waiting for transfers between devices, partner(): return lax.ppermute(block, 'tp', [(i, i ^ distance) for i in devices])  18.3 us
    ppermute x8, starting transfers between devices, onward(): return lax.ppermute(block, ('section', 'tp'), route)  13.7 us
    ppermute x8, waiting for transfers between devices, onward(): return lax.ppermute(block, ('section', 'tp'), route)  10.1 us
  transfers between devices with their start and end apart: 56, of which 16 were waited for; matrix products, arithmetic and copies ran while one was open for 0% of the time, Pallas kernels for 52%

commit v1 on v0

--- a/solution.py
+++ b/solution.py
@@ -123,11 +123,11 @@
 GU_SLOTS, DN_SLOTS = 3, 3
 GU_SPLIT, DN_SPLIT = 512, 256
 GU_PARTS = ((0, 4), (3,), (2, 1), (7, 6, 5), (3, 2, 1))
-GU_HELD = (2, 1, 2, 3, 0)
+GU_HELD = (0, 2, 2, 3, 0)
 DN_PARTS = ((5, 7), (1, 3), (4, 6, 0, 2))
 DN_HELD = (4, 4, 0)
 GU_LAST, GU_FIRST_ROUND = 3, 4
-GU_BROUGHT, GU_STAYING = (0, 1, 2), (3,)
+GU_BROUGHT, GU_STAYING = (1, 2), (3,)
 
 
 def chosen(options, nth):

time: 289 us -> 287 us (level)
  starting transfers between devices: 58 us -> 53.1 us
  waiting for transfers between devices: 28.4 us -> 32.4 us
    ppermute x48, starting transfers between devices: 44.3 us -> 40.4 us  [partner(): return lax.ppermute(block, 'tp', [(i, i ^ distance) for i in devices])]
    pallas_call x7, Pallas kernels: 49.2 us -> 45.5 us  [hold(): pl.pallas_call(functools.partial(hold_kernel, parts), in_specs=[SM] + [HB...]
    ppermute x8, waiting for transfers between devices: 10.1 us -> 13.2 us  [onward(): return lax.ppermute(block, ('section', 'tp'), route)]
  transfers between devices with their start and end apart: 56 -> 56, of which waited for: 16 -> 18; matrix products, arithmetic and copies ran while one was open for 0% -> 0% of each run, Pallas kernels for 52% -> 52%
where the time goes in v1:
time: 287 us
  Pallas kernels  196 us (68%)
  starting transfers between devices  53.1 us (19%)
  waiting for transfers between devices  32.4 us (11%)
  other arithmetic  3.59 us (1%)
    pallas_call x15, Pallas kernels, gate_up(): pl.pallas_call(functools.partial(gate_up_kernel, part, len(xs), len(befor...  93.3 us
    pallas_call x12, Pallas kernels, down(): pl.pallas_call(functools.partial(down_kernel, part, n_held), in_specs=[SM...  53.4 us
    pallas_call x7, Pallas kernels, hold(): pl.pallas_call(functools.partial(hold_kernel, parts), in_specs=[SM] + [HB...  45.5 us
    ppermute x48, starting transfers between devices, partner(): return lax.ppermute(block, 'tp', [(i, i ^ distance) for i in devices])  40.4 us
    ppermute x48, waiting for transfers between devices, partner(): return lax.ppermute(block, 'tp', [(i, i ^ distance) for i in devices])  19.2 us
    ppermute x8, waiting for transfers between devices, onward(): return lax.ppermute(block, ('section', 'tp'), route)  13.2 us
    ppermute x8, starting transfers between devices, onward(): return lax.ppermute(block, ('section', 'tp'), route)  12.8 us
  transfers between devices with their start and end apart: 56, of which 18 were waited for; matrix products, arithmetic and copies ran while one was open for 0% of the time, Pallas kernels for 52%

profile of v1, /device:TPU:0, one launch (start us, length us, event | category | flops | bytes accessed | tf_op | source)
XLA Modules:
  0.0 286.6 jit_solution(10341092076084376716)
XLA Ops:
  2.1 4.7 %collective-permute-start = (bf16[64,1152]{1,0:T(8,128)(2,1)S(1)}, bf16[64,1152]{1,0:T(8,128)(2,1)S(1)}, u32[]{:S(2)}, u32[]{:S(2)}) collective-permute-start(bf16[64,1152]{1,0:T(8,128)(2,1)S(1)} %get-tuple-element.387.x_ref), channel_id=1, source_target_pairs={{0,6},{1,7},{2,4},{3,5},{4,2},{5,3},{6,0},{7,1},{8,14},{9,15},{10,... | collective-permute-start | bytes 442376 | tf_op jit(solution)/shard_map/ppermute | solution.py:588
  8.9 7.2 %gate_up.15 = (f32[2,64,2048]{2,1,0:T(8,128)S(1)}, f32[64,128]{1,0:T(8,128)S(1)}) custom-call(s32[1]{0:T(128)} %bitcast.me_ref, s32[32]{0:T(128)S(1)} %broadcast_in_dim.61.send_ref, f32[1,8192]{1,0:T(1,128)S(1)} %get-tuple-element.176.gain_ref, f32[2,128,2048]{2,1,0:T(8,128)S(1)} %get-tuple-element.177.masks, ...), custom_call_target="tpu_custom_call" | custom-call | flops 1073741824 | bytes 16777216 | tf_op jit(solution)/shard_map/gate_up/pallas_call | solution.py:458
  16.1 3.8 %collective-permute-done.1 = bf16[64,1152]{1,0:T(8,128)(2,1)S(1)} collective-permute-done((bf16[64,1152]{1,0:T(8,128)(2,1)S(1)}, bf16[64,1152]{1,0:T(8,128)(2,1)S(1)}, u32[]{:S(2)}, u32[]{:S(2)}) %collective-permute-start.1) | collective-permute-done | bytes 147488 | tf_op jit(solution)/shard_map/ppermute | solution.py:588
  20.0 9.6 %gate_up.16 = (f32[2,64,2048]{2,1,0:T(8,128)S(1)}, f32[64,128]{1,0:T(8,128)S(1)}) custom-call(s32[1]{0:T(128)} %bitcast.me_ref, s32[32]{0:T(128)S(1)} %broadcast_in_dim.61.send_ref, f32[1,8192]{1,0:T(1,128)S(1)} %get-tuple-element.176.gain_ref, f32[2,128,2048]{2,1,0:T(8,128)S(1)} %get-tuple-element.177.masks, bf16[1,64,1152]{2,1,0:T(8,128)(2,1)S(1)} %bitcast.104, ...), custom_call_target="tpu_custom_call" | custom-call | flops 1610612736 | bytes 25165824 | tf_op jit(solution)/shard_map/gate_up/pallas_call | solution.py:458
  32.1 10.1 %gate_up.17 = bf16[8,64,256]{2,1,0:T(8,128)(2,1)S(1)} custom-call(s32[1]{0:T(128)} %bitcast.me_ref, s32[32]{0:T(128)S(1)} %get-tuple-element.189.send_ref, f32[1,8192]{1,0:T(1,128)S(1)} %get-tuple-element.176.gain_ref, f32[2,128,2048]{2,1,0:T(8,128)S(1)} %get-tuple-element.177.masks, bf16[3,64,1152]{2,1,0:T(8,128)(2,1)S(1)} %collective-permute-done.4.refs_3_.refs_0_, ...), custom_call_target="tpu_custom_call" | custom-call | flops 1610612736 | bytes 25165824 | tf_op jit(solution)/shard_map/gate_up/pallas_call | solution.py:458
  44.0 3.0 %collective-permute-start.7 = (bf16[64,512]{1,0:T(8,128)(2,1)S(1)}, bf16[64,512]{1,0:T(8,128)(2,1)S(1)}, u32[]{:S(2)}, u32[]{:S(2)}) collective-permute-start(bf16[64,512]{1,0:T(8,128)(2,1)S(1)} %get-tuple-element.382), channel_id=1, source_target_pairs={{0,4},{1,5},{2,6},{3,7},{4,0},{5,1},{6,2},{7,3},{8,12},{9,13},{10,... | collective-permute-start | bytes 196616 | tf_op jit(solution)/shard_map/ppermute | solution.py:588
  48.4 6.0 %hold.7 = (bf16[4,2048,512]{2,1,0:T(8,128)(2,1)S(1)}, bf16[4,2048,512]{2,1,0:T(8,128)(2,1)S(1)}) custom-call(s32[1]{0:T(128)} %bitcast.me_ref, bf16[1,2048,8192]{2,1,0:T(8,128)(2,1)} %refs_0_.21), custom_call_target="tpu_custom_call" | custom-call | bytes 16777216 | tf_op jit(solution)/shard_map/hold/pallas_call | solution.py:302
  54.5 3.1 %down.12 = (bf16[2,64,1024]{2,1,0:T(8,128)(2,1)S(1)}, bf16[64,2048]{1,0:T(8,128)(2,1)S(1)}) custom-call(s32[1]{0:T(128)} %bitcast.me_ref, s32[32]{0:T(128)S(1)} %get-tuple-element.188.take_ref, bf16[8,64,256]{2,1,0:T(8,128)(2,1)S(1)} %pad_maximum_fusion.6.inner_ref, bf16[64,1152]{1,0:T(8,128)(2,1)S(1)} %get-tuple-element.387.x_ref, ...), custom_call_target="tpu_custom_call" | custom-call | flops 536870912 | tf_op jit(solution)/shard_map/down/pallas_call | solution.py:567
  60.5 7.6 %down.14 = (f32[4,64,1024]{2,1,0:T(8,128)S(1)}, bf16[2,64,1024]{2,1,0:T(8,128)(2,1)S(1)}) custom-call(s32[1]{0:T(128)} %bitcast.me_ref, s32[32]{0:T(128)S(1)} %get-tuple-element.188.take_ref, bf16[64,2048]{1,0:T(8,128)(2,1)S(1)} %get-tuple-element.206.inner_ref, bf16[64,1152]{1,0:T(8,128)(2,1)S(1)} %get-tuple-element.387.x_ref, ...), custom_call_target="tpu_custom_call" | custom-call | flops 1073741824 | bytes 16777216 | tf_op jit(solution)/shard_map/down/pallas_call | solution.py:567
  70.8 3.0 %collective-permute-start.12 = (bf16[64,1024]{1,0:T(8,128)(2,1)S(1)}, bf16[64,1024]{1,0:T(8,128)(2,1)S(1)}, u32[]{:S(2)}, u32[]{:S(2)}) collective-permute-start(bf16[64,1024]{1,0:T(8,128)(2,1)S(1)} %get-tuple-element.378), channel_id=1, source_target_pairs={{0,12},{1,13},{2,14},{3,15},{4,8},{5,9},{6,10},{7,11},{8,20},{9,21... | collective-permute-start | bytes 393224 | tf_op jit(solution)/shard_map/ppermute | solution.py:599
  75.4 9.6 %hold.8 = (bf16[2,2,512,2048]{3,2,1,0:T(8,128)(2,1)S(1)}, bf16[2,2,512,2048]{3,2,1,0:T(8,128)(2,1)S(1)}, bf16[3,2,512,2048]{3,2,1,0:T(8,128)(2,1)S(1)}) custom-call(s32[1]{0:T(128)} %bitcast.me_ref, bf16[1,8192,2048]{2,1,0:T(8,128)(2,1)} %refs_4_.13, bf16[1,8192,2048]{2,1,0:T(8,128)(2,1)} %refs_5_.19), custom_call_target="tpu_custom_call" | custom-call | bytes 29360128 | tf_op jit(solution)/shard_map/hold/pallas_call | solution.py:302
  89.5 7.2 %gate_up.18 = (f32[2,64,2048]{2,1,0:T(8,128)S(1)}, f32[64,128]{1,0:T(8,128)S(1)}) custom-call(s32[1]{0:T(128)} %bitcast.me_ref, s32[32]{0:T(128)S(1)} %get-tuple-element.189.send_ref, f32[1,8192]{1,0:T(1,128)S(1)} %get-tuple-element.176.gain_ref, f32[2,128,2048]{2,1,0:T(8,128)S(1)} %get-tuple-element.177.masks, bf16[1,64,1024]{2,1,0:T(8,128)(2,1)S(1)} %bitcast.100, ...), custom_call_target="tpu_custom_call" | custom-call | flops 1073741824 | bytes 16777216 | tf_op jit(solution)/shard_map/gate_up/pallas_call | solution.py:458
  100.0 5.1 %gate_up.20 = (f32[2,64,2048]{2,1,0:T(8,128)S(1)}, f32[64,128]{1,0:T(8,128)S(1)}) custom-call(s32[1]{0:T(128)} %bitcast.me_ref, s32[32]{0:T(128)S(1)} %get-tuple-element.189.send_ref, f32[1,8192]{1,0:T(1,128)S(1)} %get-tuple-element.176.gain_ref, f32[2,128,2048]{2,1,0:T(8,128)S(1)} %get-tuple-element.177.masks, bf16[1,64,1024]{2,1,0:T(8,128)(2,1)S(1)} %bitcast.112, ...), custom_call_target="tpu_custom_call" | custom-call | flops 1073741824 | bytes 8388608 | tf_op jit(solution)/shard_map/gate_up/pallas_call | solution.py:458
  105.1 7.4 %gate_up.21 = bf16[8,64,256]{2,1,0:T(8,128)(2,1)S(1)} custom-call(s32[1]{0:T(128)} %bitcast.me_ref, s32[32]{0:T(128)S(1)} %get-tuple-element.189.send_ref, f32[1,8192]{1,0:T(1,128)S(1)} %get-tuple-element.176.gain_ref, f32[2,128,2048]{2,1,0:T(8,128)S(1)} %get-tuple-element.177.masks, bf16[3,64,1024]{2,1,0:T(8,128)(2,1)S(1)} %collective-permute-done.18.refs_0_, ...), custom_call_target="tpu_custom_call" | custom-call | flops 1610612736 | bytes 12582912 | tf_op jit(solution)/shard_map/gate_up/pallas_call | solution.py:458
  118.6 6.0 %hold.9 = (bf16[4,2048,512]{2,1,0:T(8,128)(2,1)S(1)}, bf16[4,2048,512]{2,1,0:T(8,128)(2,1)S(1)}) custom-call(s32[1]{0:T(128)} %bitcast.me_ref, bf16[1,2048,8192]{2,1,0:T(8,128)(2,1)} %refs_0_.21), custom_call_target="tpu_custom_call" | custom-call | bytes 16777216 | tf_op jit(solution)/shard_map/hold/pallas_call | solution.py:302
  124.8 3.1 %down.15 = (bf16[2,64,1024]{2,1,0:T(8,128)(2,1)S(1)}, bf16[64,2048]{1,0:T(8,128)(2,1)S(1)}) custom-call(s32[1]{0:T(128)} %bitcast.me_ref, s32[32]{0:T(128)S(1)} %get-tuple-element.188.take_ref, bf16[8,64,256]{2,1,0:T(8,128)(2,1)S(1)} %pad_maximum_fusion.9.inner_ref, bf16[64,1024]{1,0:T(8,128)(2,1)S(1)} %add_convert_fusion.11.x_ref, ...), custom_call_target="tpu_custom_call" | custom-call | flops 536870912 | tf_op jit(solution)/shard_map/down/pallas_call | solution.py:567
  130.8 7.6 %down.17 = (f32[4,64,1024]{2,1,0:T(8,128)S(1)}, bf16[2,64,1024]{2,1,0:T(8,128)(2,1)S(1)}) custom-call(s32[1]{0:T(128)} %bitcast.me_ref, s32[32]{0:T(128)S(1)} %get-tuple-element.188.take_ref, bf16[64,2048]{1,0:T(8,128)(2,1)S(1)} %get-tuple-element.252.inner_ref, bf16[64,1024]{1,0:T(8,128)(2,1)S(1)} %add_convert_fusion.11.x_ref, ...), custom_call_target="tpu_custom_call" | custom-call | flops 1073741824 | bytes 16777216 | tf_op jit(solution)/shard_map/down/pallas_call | solution.py:567
  143.5 5.9 %hold.10 = (bf16[2,2,512,2048]{3,2,1,0:T(8,128)(2,1)S(1)}, bf16[2,2,512,2048]{3,2,1,0:T(8,128)(2,1)S(1)}) custom-call(s32[1]{0:T(128)} %bitcast.me_ref, bf16[1,8192,2048]{2,1,0:T(8,128)(2,1)} %refs_4_.13, bf16[1,8192,2048]{2,1,0:T(8,128)(2,1)} %refs_5_.19), custom_call_target="tpu_custom_call" | custom-call | bytes 16777216 | tf_op jit(solution)/shard_map/hold/pallas_call | solution.py:302
  156.8 7.2 %gate_up.22 = (f32[2,64,2048]{2,1,0:T(8,128)S(1)}, f32[64,128]{1,0:T(8,128)S(1)}) custom-call(s32[1]{0:T(128)} %bitcast.me_ref, s32[32]{0:T(128)S(1)} %get-tuple-element.189.send_ref, f32[1,8192]{1,0:T(1,128)S(1)} %get-tuple-element.176.gain_ref, f32[2,128,2048]{2,1,0:T(8,128)S(1)} %get-tuple-element.177.masks, bf16[1,64,1024]{2,1,0:T(8,128)(2,1)S(1)} %bitcast.101, ...), custom_call_target="tpu_custom_call" | custom-call | flops 1073741824 | bytes 16777216 | tf_op jit(solution)/shard_map/gate_up/pallas_call | solution.py:458
  167.0 5.1 %gate_up.24 = (f32[2,64,2048]{2,1,0:T(8,128)S(1)}, f32[64,128]{1,0:T(8,128)S(1)}) custom-call(s32[1]{0:T(128)} %bitcast.me_ref, s32[32]{0:T(128)S(1)} %get-tuple-element.189.send_ref, f32[1,8192]{1,0:T(1,128)S(1)} %get-tuple-element.176.gain_ref, f32[2,128,2048]{2,1,0:T(8,128)S(1)} %get-tuple-element.177.masks, bf16[1,64,1024]{2,1,0:T(8,128)(2,1)S(1)} %bitcast.114, ...), custom_call_target="tpu_custom_call" | custom-call | flops 1073741824 | bytes 8388608 | tf_op jit(solution)/shard_map/gate_up/pallas_call | solution.py:458
  172.2 7.4 %gate_up.25 = bf16[8,64,256]{2,1,0:T(8,128)(2,1)S(1)} custom-call(s32[1]{0:T(128)} %bitcast.me_ref, s32[32]{0:T(128)S(1)} %get-tuple-element.189.send_ref, f32[1,8192]{1,0:T(1,128)S(1)} %get-tuple-element.176.gain_ref, f32[2,128,2048]{2,1,0:T(8,128)S(1)} %get-tuple-element.177.masks, bf16[3,64,1024]{2,1,0:T(8,128)(2,1)S(1)} %collective-permute-done.32.refs_0_, ...), custom_call_target="tpu_custom_call" | custom-call | flops 1610612736 | bytes 12582912 | tf_op jit(solution)/shard_map/gate_up/pallas_call | solution.py:458
  185.6 6.0 %hold.11 = (bf16[4,2048,512]{2,1,0:T(8,128)(2,1)S(1)}, bf16[4,2048,512]{2,1,0:T(8,128)(2,1)S(1)}) custom-call(s32[1]{0:T(128)} %bitcast.me_ref, bf16[1,2048,8192]{2,1,0:T(8,128)(2,1)} %refs_0_.21), custom_call_target="tpu_custom_call" | custom-call | bytes 16777216 | tf_op jit(solution)/shard_map/hold/pallas_call | solution.py:302
  191.8 3.1 %down.18 = (bf16[2,64,1024]{2,1,0:T(8,128)(2,1)S(1)}, bf16[64,2048]{1,0:T(8,128)(2,1)S(1)}) custom-call(s32[1]{0:T(128)} %bitcast.me_ref, s32[32]{0:T(128)S(1)} %get-tuple-element.188.take_ref, bf16[8,64,256]{2,1,0:T(8,128)(2,1)S(1)} %pad_maximum_fusion.12.inner_ref, bf16[64,1024]{1,0:T(8,128)(2,1)S(1)} %add_convert_fusion.10.x_ref, ...), custom_call_target="tpu_custom_call" | custom-call | flops 536870912 | tf_op jit(solution)/shard_map/down/pallas_call | solution.py:567
  197.8 7.6 %down.20 = (f32[4,64,1024]{2,1,0:T(8,128)S(1)}, bf16[2,64,1024]{2,1,0:T(8,128)(2,1)S(1)}) custom-call(s32[1]{0:T(128)} %bitcast.me_ref, s32[32]{0:T(128)S(1)} %get-tuple-element.188.take_ref, bf16[64,2048]{1,0:T(8,128)(2,1)S(1)} %get-tuple-element.296.inner_ref, bf16[64,1024]{1,0:T(8,128)(2,1)S(1)} %add_convert_fusion.10.x_ref, ...), custom_call_target="tpu_custom_call" | custom-call | flops 1073741824 | bytes 16777216 | tf_op jit(solution)/shard_map/down/pallas_call | solution.py:567
  211.0 5.9 %hold.12 = (bf16[2,2,512,2048]{3,2,1,0:T(8,128)(2,1)S(1)}, bf16[2,2,512,2048]{3,2,1,0:T(8,128)(2,1)S(1)}) custom-call(s32[1]{0:T(128)} %bitcast.me_ref, bf16[1,8192,2048]{2,1,0:T(8,128)(2,1)} %refs_4_.13, bf16[1,8192,2048]{2,1,0:T(8,128)(2,1)} %refs_5_.19), custom_call_target="tpu_custom_call" | custom-call | bytes 16777216 | tf_op jit(solution)/shard_map/hold/pallas_call | solution.py:302
  223.8 7.2 %gate_up.26 = (f32[2,64,2048]{2,1,0:T(8,128)S(1)}, f32[64,128]{1,0:T(8,128)S(1)}) custom-call(s32[1]{0:T(128)} %bitcast.me_ref, s32[32]{0:T(128)S(1)} %get-tuple-element.189.send_ref, f32[1,8192]{1,0:T(1,128)S(1)} %get-tuple-element.176.gain_ref, f32[2,128,2048]{2,1,0:T(8,128)S(1)} %get-tuple-element.177.masks, bf16[1,64,1024]{2,1,0:T(8,128)(2,1)S(1)} %bitcast.102, ...), custom_call_target="tpu_custom_call" | custom-call | flops 1073741824 | bytes 16777216 | tf_op jit(solution)/shard_map/gate_up/pallas_call | solution.py:458
  233.6 5.1 %gate_up.28 = (f32[2,64,2048]{2,1,0:T(8,128)S(1)}, f32[64,128]{1,0:T(8,128)S(1)}) custom-call(s32[1]{0:T(128)} %bitcast.me_ref, s32[32]{0:T(128)S(1)} %get-tuple-element.189.send_ref, f32[1,8192]{1,0:T(1,128)S(1)} %get-tuple-element.176.gain_ref, f32[2,128,2048]{2,1,0:T(8,128)S(1)} %get-tuple-element.177.masks, bf16[1,64,1024]{2,1,0:T(8,128)(2,1)S(1)} %bitcast.116, ...), custom_call_target="tpu_custom_call" | custom-call | flops 1073741824 | bytes 8388608 | tf_op jit(solution)/shard_map/gate_up/pallas_call | solution.py:458
  238.8 7.4 %gate_up.29 = bf16[8,64,256]{2,1,0:T(8,128)(2,1)S(1)} custom-call(s32[1]{0:T(128)} %bitcast.me_ref, s32[32]{0:T(128)S(1)} %get-tuple-element.189.send_ref, f32[1,8192]{1,0:T(1,128)S(1)} %get-tuple-element.176.gain_ref, f32[2,128,2048]{2,1,0:T(8,128)S(1)} %get-tuple-element.177.masks, bf16[3,64,1024]{2,1,0:T(8,128)(2,1)S(1)} %collective-permute-done.46.refs_0_, ...), custom_call_target="tpu_custom_call" | custom-call | flops 1610612736 | bytes 12582912 | tf_op jit(solution)/shard_map/gate_up/pallas_call | solution.py:458
  252.2 6.0 %hold.13 = (bf16[4,2048,512]{2,1,0:T(8,128)(2,1)S(1)}, bf16[4,2048,512]{2,1,0:T(8,128)(2,1)S(1)}) custom-call(s32[1]{0:T(128)} %bitcast.me_ref, bf16[1,2048,8192]{2,1,0:T(8,128)(2,1)} %refs_0_.21), custom_call_target="tpu_custom_call" | custom-call | bytes 16777216 | tf_op jit(solution)/shard_map/hold/pallas_call | solution.py:302
  258.4 3.1 %down.21 = (bf16[2,64,1024]{2,1,0:T(8,128)(2,1)S(1)}, bf16[64,2048]{1,0:T(8,128)(2,1)S(1)}) custom-call(s32[1]{0:T(128)} %bitcast.me_ref, s32[32]{0:T(128)S(1)} %get-tuple-element.188.take_ref, bf16[8,64,256]{2,1,0:T(8,128)(2,1)S(1)} %pad_maximum_fusion.15.inner_ref, bf16[64,1024]{1,0:T(8,128)(2,1)S(1)} %add_convert_fusion.9.x_ref, ...), custom_call_target="tpu_custom_call" | custom-call | flops 536870912 | tf_op jit(solution)/shard_map/down/pallas_call | solution.py:567
  264.4 7.6 %down.23 = (f32[4,64,1024]{2,1,0:T(8,128)S(1)}, bf16[2,64,1024]{2,1,0:T(8,128)(2,1)S(1)}) custom-call(s32[1]{0:T(128)} %bitcast.me_ref, s32[32]{0:T(128)S(1)} %get-tuple-element.188.take_ref, bf16[64,2048]{1,0:T(8,128)(2,1)S(1)} %get-tuple-element.340.inner_ref, bf16[64,1024]{1,0:T(8,128)(2,1)S(1)} %add_convert_fusion.9.x_ref, ...), custom_call_target="tpu_custom_call" | custom-call | flops 1073741824 | bytes 16777216 | tf_op jit(solution)/shard_map/down/pallas_call | solution.py:567
  277.8 8.1 %collective-permute-done.54 = bf16[64,1024]{1,0:T(8,128)(2,1)S(1)} collective-permute-done((bf16[64,1024]{1,0:T(8,128)(2,1)S(1)}, bf16[64,1024]{1,0:T(8,128)(2,1)S(1)}, u32[]{:S(2)}, u32[]{:S(2)}) %collective-permute-start.54) | collective-permute-done | bytes 131104 | tf_op jit(solution)/shard_map/ppermute | solution.py:599
  (172 shorter events, 88.5 us)
Async XLA Ops:
  2.1 14.0 %collective-permute-start = (bf16[64,1152]{1,0:T(8,128)(2,1)S(1)}, bf16[64,1152]{1,0:T(8,128)(2,1)S(1)}, u32[]{:S(2)}, u32[]{:S(2)}) collective-permute-start(bf16[64,1152]{1,0:T(8,128)(2,1)S(1)} %get-tuple-element.387.x_ref), channel_id=1, source_target_pairs={{0,6},{1,7},{2,4},{3,5},{4,2},{5,3},{6,0},{7,1},{8,14},{9,15},{10,... | collective-permute-start | bytes 442376 | tf_op jit(solution)/shard_map/ppermute | solution.py:588
  6.8 13.1 %collective-permute-start.1 = (bf16[64,1152]{1,0:T(8,128)(2,1)S(1)}, bf16[64,1152]{1,0:T(8,128)(2,1)S(1)}, u32[]{:S(2)}, u32[]{:S(2)}) collective-permute-start(bf16[64,1152]{1,0:T(8,128)(2,1)S(1)} %get-tuple-element.387.x_ref), channel_id=1, source_target_pairs={{0,4},{1,5},{2,6},{3,7},{4,0},{5,1},{6,2},{7,3},{8,12},{9,13},{10,... | collective-permute-start | bytes 442376 | tf_op jit(solution)/shard_map/ppermute | solution.py:588
  6.8 13.1 %collective-permute-start.2 = (bf16[64,1152]{1,0:T(8,128)(2,1)S(1)}, bf16[64,1152]{1,0:T(8,128)(2,1)S(1)}, u32[]{:S(2)}, u32[]{:S(2)}) collective-permute-start(bf16[64,1152]{1,0:T(8,128)(2,1)S(1)} %get-tuple-element.387.x_ref), channel_id=1, source_target_pairs={{0,2},{1,3},{2,0},{3,1},{4,6},{5,7},{6,4},{7,5},{8,10},{9,11},{10,... | collective-permute-start | bytes 442376 | tf_op jit(solution)/shard_map/ppermute | solution.py:588
  20.0 9.7 %collective-permute-start.4 = (bf16[3,64,1152]{2,1,0:T(8,128)(2,1)S(1)}, bf16[3,64,1152]{2,1,0:T(8,128)(2,1)S(1)}, u32[]{:S(2)}, u32[]{:S(2)}) collective-permute-start(bf16[3,64,1152]{2,1,0:T(8,128)(2,1)S(1)} %pad_maximum_fusion.refs_1_), channel_id=1, source_target_pairs={{0,1},{1,0},{2,3},{3,2},{4,5},{5,4},{6,7},{7,6},{8,9},{9,8},{10,11... | collective-permute-start | bytes 1327112 | tf_op jit(solution)/shard_map/ppermute | solution.py:588
  43.9 10.5 %collective-permute-start.6 = (bf16[64,512]{1,0:T(8,128)(2,1)S(1)}, bf16[64,512]{1,0:T(8,128)(2,1)S(1)}, u32[]{:S(2)}, u32[]{:S(2)}) collective-permute-start(bf16[64,512]{1,0:T(8,128)(2,1)S(1)} %get-tuple-element.383), channel_id=1, source_target_pairs={{0,2},{1,3},{2,0},{3,1},{4,6},{5,7},{6,4},{7,5},{8,10},{9,11},{10,... | collective-permute-start | bytes 196616 | tf_op jit(solution)/shard_map/ppermute | solution.py:588
  44.0 10.4 %collective-permute-start.7 = (bf16[64,512]{1,0:T(8,128)(2,1)S(1)}, bf16[64,512]{1,0:T(8,128)(2,1)S(1)}, u32[]{:S(2)}, u32[]{:S(2)}) collective-permute-start(bf16[64,512]{1,0:T(8,128)(2,1)S(1)} %get-tuple-element.382), channel_id=1, source_target_pairs={{0,4},{1,5},{2,6},{3,7},{4,0},{5,1},{6,2},{7,3},{8,12},{9,13},{10,... | collective-permute-start | bytes 196616 | tf_op jit(solution)/shard_map/ppermute | solution.py:588
  60.4 8.8 %collective-permute-start.10 = (bf16[2,64,1024]{2,1,0:T(8,128)(2,1)S(1)}, bf16[2,64,1024]{2,1,0:T(8,128)(2,1)S(1)}, u32[]{:S(2)}, u32[]{:S(2)}) collective-permute-start(bf16[2,64,1024]{2,1,0:T(8,128)(2,1)S(1)} %add_convert_fusion.7), channel_id=1, source_target_pairs={{0,2},{1,3},{2,0},{3,1},{4,6},{5,7},{6,4},{7,5},{8,10},{9,11},{10,... | collective-permute-start | bytes 786440 | tf_op jit(solution)/shard_map/ppermute | solution.py:588
  70.8 14.1 %collective-permute-start.12 = (bf16[64,1024]{1,0:T(8,128)(2,1)S(1)}, bf16[64,1024]{1,0:T(8,128)(2,1)S(1)}, u32[]{:S(2)}, u32[]{:S(2)}) collective-permute-start(bf16[64,1024]{1,0:T(8,128)(2,1)S(1)} %get-tuple-element.378), channel_id=1, source_target_pairs={{0,12},{1,13},{2,14},{3,15},{4,8},{5,9},{6,10},{7,11},{8,20},{9,21... | collective-permute-start | bytes 393224 | tf_op jit(solution)/shard_map/ppermute | solution.py:599
  73.9 11.1 %collective-permute-start.13 = (bf16[64,1024]{1,0:T(8,128)(2,1)S(1)}, bf16[64,1024]{1,0:T(8,128)(2,1)S(1)}, u32[]{:S(2)}, u32[]{:S(2)}) collective-permute-start(bf16[64,1024]{1,0:T(8,128)(2,1)S(1)} %get-tuple-element.377), channel_id=1, source_target_pairs={{0,8},{1,9},{2,10},{3,11},{4,12},{5,13},{6,14},{7,15},{8,16},{9,17... | collective-permute-start | bytes 393224 | tf_op jit(solution)/shard_map/ppermute | solution.py:599
  85.1 11.7 %collective-permute-start.14 = (bf16[64,1024]{1,0:T(8,128)(2,1)S(1)}, bf16[64,1024]{1,0:T(8,128)(2,1)S(1)}, u32[]{:S(2)}, u32[]{:S(2)}) collective-permute-start(bf16[64,1024]{1,0:T(8,128)(2,1)S(1)} %add_convert_fusion.11.x_ref), channel_id=1, source_target_pairs={{0,6},{1,7},{2,4},{3,5},{4,2},{5,3},{6,0},{7,1},{8,14},{9,15},{10,... | collective-permute-start | bytes 393224 | tf_op jit(solution)/shard_map/ppermute | solution.py:588
  86.5 13.3 %collective-permute-start.16 = (bf16[64,1024]{1,0:T(8,128)(2,1)S(1)}, bf16[64,1024]{1,0:T(8,128)(2,1)S(1)}, u32[]{:S(2)}, u32[]{:S(2)}) collective-permute-start(bf16[64,1024]{1,0:T(8,128)(2,1)S(1)} %add_convert_fusion.11.x_ref), channel_id=1, source_target_pairs={{0,4},{1,5},{2,6},{3,7},{4,0},{5,1},{6,2},{7,3},{8,12},{9,13},{10,... | collective-permute-start | bytes 393224 | tf_op jit(solution)/shard_map/ppermute | solution.py:588
  87.6 12.3 %collective-permute-start.17 = (bf16[64,1024]{1,0:T(8,128)(2,1)S(1)}, bf16[64,1024]{1,0:T(8,128)(2,1)S(1)}, u32[]{:S(2)}, u32[]{:S(2)}) collective-permute-start(bf16[64,1024]{1,0:T(8,128)(2,1)S(1)} %add_convert_fusion.11.x_ref), channel_id=1, source_target_pairs={{0,2},{1,3},{2,0},{3,1},{4,6},{5,7},{6,4},{7,5},{8,10},{9,11},{10,... | collective-permute-start | bytes 393224 | tf_op jit(solution)/shard_map/ppermute | solution.py:588
  114.2 10.5 %collective-permute-start.20 = (bf16[64,512]{1,0:T(8,128)(2,1)S(1)}, bf16[64,512]{1,0:T(8,128)(2,1)S(1)}, u32[]{:S(2)}, u32[]{:S(2)}) collective-permute-start(bf16[64,512]{1,0:T(8,128)(2,1)S(1)} %get-tuple-element.373), channel_id=1, source_target_pairs={{0,2},{1,3},{2,0},{3,1},{4,6},{5,7},{6,4},{7,5},{8,10},{9,11},{10,... | collective-permute-start | bytes 196616 | tf_op jit(solution)/shard_map/ppermute | solution.py:588
  114.9 9.8 %collective-permute-start.21 = (bf16[64,512]{1,0:T(8,128)(2,1)S(1)}, bf16[64,512]{1,0:T(8,128)(2,1)S(1)}, u32[]{:S(2)}, u32[]{:S(2)}) collective-permute-start(bf16[64,512]{1,0:T(8,128)(2,1)S(1)} %get-tuple-element.372), channel_id=1, source_target_pairs={{0,4},{1,5},{2,6},{3,7},{4,0},{5,1},{6,2},{7,3},{8,12},{9,13},{10,... | collective-permute-start | bytes 196616 | tf_op jit(solution)/shard_map/ppermute | solution.py:588
  130.7 8.8 %collective-permute-start.24 = (bf16[2,64,1024]{2,1,0:T(8,128)(2,1)S(1)}, bf16[2,64,1024]{2,1,0:T(8,128)(2,1)S(1)}, u32[]{:S(2)}, u32[]{:S(2)}) collective-permute-start(bf16[2,64,1024]{2,1,0:T(8,128)(2,1)S(1)} %add_convert_fusion.5), channel_id=1, source_target_pairs={{0,2},{1,3},{2,0},{3,1},{4,6},{5,7},{6,4},{7,5},{8,10},{9,11},{10,... | collective-permute-start | bytes 786440 | tf_op jit(solution)/shard_map/ppermute | solution.py:588
  141.1 11.1 %collective-permute-start.26 = (bf16[64,1024]{1,0:T(8,128)(2,1)S(1)}, bf16[64,1024]{1,0:T(8,128)(2,1)S(1)}, u32[]{:S(2)}, u32[]{:S(2)}) collective-permute-start(bf16[64,1024]{1,0:T(8,128)(2,1)S(1)} %get-tuple-element.368), channel_id=1, source_target_pairs={{0,12},{1,13},{2,14},{3,15},{4,8},{5,9},{6,10},{7,11},{8,20},{9,21... | collective-permute-start | bytes 393224 | tf_op jit(solution)/shard_map/ppermute | solution.py:599
  143.0 9.2 %collective-permute-start.27 = (bf16[64,1024]{1,0:T(8,128)(2,1)S(1)}, bf16[64,1024]{1,0:T(8,128)(2,1)S(1)}, u32[]{:S(2)}, u32[]{:S(2)}) collective-permute-start(bf16[64,1024]{1,0:T(8,128)(2,1)S(1)} %get-tuple-element.367), channel_id=1, source_target_pairs={{0,8},{1,9},{2,10},{3,11},{4,12},{5,13},{6,14},{7,15},{8,16},{9,17... | collective-permute-start | bytes 393224 | tf_op jit(solution)/shard_map/ppermute | solution.py:599
  152.3 11.7 %collective-permute-start.28 = (bf16[64,1024]{1,0:T(8,128)(2,1)S(1)}, bf16[64,1024]{1,0:T(8,128)(2,1)S(1)}, u32[]{:S(2)}, u32[]{:S(2)}) collective-permute-start(bf16[64,1024]{1,0:T(8,128)(2,1)S(1)} %add_convert_fusion.10.x_ref), channel_id=1, source_target_pairs={{0,6},{1,7},{2,4},{3,5},{4,2},{5,3},{6,0},{7,1},{8,14},{9,15},{10,... | collective-permute-start | bytes 393224 | tf_op jit(solution)/shard_map/ppermute | solution.py:588
  154.1 12.8 %collective-permute-start.30 = (bf16[64,1024]{1,0:T(8,128)(2,1)S(1)}, bf16[64,1024]{1,0:T(8,128)(2,1)S(1)}, u32[]{:S(2)}, u32[]{:S(2)}) collective-permute-start(bf16[64,1024]{1,0:T(8,128)(2,1)S(1)} %add_convert_fusion.10.x_ref), channel_id=1, source_target_pairs={{0,4},{1,5},{2,6},{3,7},{4,0},{5,1},{6,2},{7,3},{8,12},{9,13},{10,... | collective-permute-start | bytes 393224 | tf_op jit(solution)/shard_map/ppermute | solution.py:588
  154.6 12.3 %collective-permute-start.31 = (bf16[64,1024]{1,0:T(8,128)(2,1)S(1)}, bf16[64,1024]{1,0:T(8,128)(2,1)S(1)}, u32[]{:S(2)}, u32[]{:S(2)}) collective-permute-start(bf16[64,1024]{1,0:T(8,128)(2,1)S(1)} %add_convert_fusion.10.x_ref), channel_id=1, source_target_pairs={{0,2},{1,3},{2,0},{3,1},{4,6},{5,7},{6,4},{7,5},{8,10},{9,11},{10,... | collective-permute-start | bytes 393224 | tf_op jit(solution)/shard_map/ppermute | solution.py:588
  181.2 10.5 %collective-permute-start.34 = (bf16[64,512]{1,0:T(8,128)(2,1)S(1)}, bf16[64,512]{1,0:T(8,128)(2,1)S(1)}, u32[]{:S(2)}, u32[]{:S(2)}) collective-permute-start(bf16[64,512]{1,0:T(8,128)(2,1)S(1)} %get-tuple-element.363), channel_id=1, source_target_pairs={{0,2},{1,3},{2,0},{3,1},{4,6},{5,7},{6,4},{7,5},{8,10},{9,11},{10,... | collective-permute-start | bytes 196616 | tf_op jit(solution)/shard_map/ppermute | solution.py:588
  181.9 9.8 %collective-permute-start.35 = (bf16[64,512]{1,0:T(8,128)(2,1)S(1)}, bf16[64,512]{1,0:T(8,128)(2,1)S(1)}, u32[]{:S(2)}, u32[]{:S(2)}) collective-permute-start(bf16[64,512]{1,0:T(8,128)(2,1)S(1)} %get-tuple-element.362), channel_id=1, source_target_pairs={{0,4},{1,5},{2,6},{3,7},{4,0},{5,1},{6,2},{7,3},{8,12},{9,13},{10,... | collective-permute-start | bytes 196616 | tf_op jit(solution)/shard_map/ppermute | solution.py:588
  197.7 8.8 %collective-permute-start.38 = (bf16[2,64,1024]{2,1,0:T(8,128)(2,1)S(1)}, bf16[2,64,1024]{2,1,0:T(8,128)(2,1)S(1)}, u32[]{:S(2)}, u32[]{:S(2)}) collective-permute-start(bf16[2,64,1024]{2,1,0:T(8,128)(2,1)S(1)} %add_convert_fusion.3), channel_id=1, source_target_pairs={{0,2},{1,3},{2,0},{3,1},{4,6},{5,7},{6,4},{7,5},{8,10},{9,11},{10,... | collective-permute-start | bytes 786440 | tf_op jit(solution)/shard_map/ppermute | solution.py:588
  208.1 11.1 %collective-permute-start.40 = (bf16[64,1024]{1,0:T(8,128)(2,1)S(1)}, bf16[64,1024]{1,0:T(8,128)(2,1)S(1)}, u32[]{:S(2)}, u32[]{:S(2)}) collective-permute-start(bf16[64,1024]{1,0:T(8,128)(2,1)S(1)} %get-tuple-element.358), channel_id=1, source_target_pairs={{0,12},{1,13},{2,14},{3,15},{4,8},{5,9},{6,10},{7,11},{8,20},{9,21... | collective-permute-start | bytes 393224 | tf_op jit(solution)/shard_map/ppermute | solution.py:599
  209.3 10.0 %collective-permute-start.41 = (bf16[64,1024]{1,0:T(8,128)(2,1)S(1)}, bf16[64,1024]{1,0:T(8,128)(2,1)S(1)}, u32[]{:S(2)}, u32[]{:S(2)}) collective-permute-start(bf16[64,1024]{1,0:T(8,128)(2,1)S(1)} %get-tuple-element.357), channel_id=1, source_target_pairs={{0,8},{1,9},{2,10},{3,11},{4,12},{5,13},{6,14},{7,15},{8,16},{9,17... | collective-permute-start | bytes 393224 | tf_op jit(solution)/shard_map/ppermute | solution.py:599
  219.3 11.7 %collective-permute-start.42 = (bf16[64,1024]{1,0:T(8,128)(2,1)S(1)}, bf16[64,1024]{1,0:T(8,128)(2,1)S(1)}, u32[]{:S(2)}, u32[]{:S(2)}) collective-permute-start(bf16[64,1024]{1,0:T(8,128)(2,1)S(1)} %add_convert_fusion.9.x_ref), channel_id=1, source_target_pairs={{0,6},{1,7},{2,4},{3,5},{4,2},{5,3},{6,0},{7,1},{8,14},{9,15},{10,... | collective-permute-start | bytes 393224 | tf_op jit(solution)/shard_map/ppermute | solution.py:588
  221.2 12.2 %collective-permute-start.44 = (bf16[64,1024]{1,0:T(8,128)(2,1)S(1)}, bf16[64,1024]{1,0:T(8,128)(2,1)S(1)}, u32[]{:S(2)}, u32[]{:S(2)}) collective-permute-start(bf16[64,1024]{1,0:T(8,128)(2,1)S(1)} %add_convert_fusion.9.x_ref), channel_id=1, source_target_pairs={{0,4},{1,5},{2,6},{3,7},{4,0},{5,1},{6,2},{7,3},{8,12},{9,13},{10,... | collective-permute-start | bytes 393224 | tf_op jit(solution)/shard_map/ppermute | solution.py:588
  221.2 12.2 %collective-permute-start.45 = (bf16[64,1024]{1,0:T(8,128)(2,1)S(1)}, bf16[64,1024]{1,0:T(8,128)(2,1)S(1)}, u32[]{:S(2)}, u32[]{:S(2)}) collective-permute-start(bf16[64,1024]{1,0:T(8,128)(2,1)S(1)} %add_convert_fusion.9.x_ref), channel_id=1, source_target_pairs={{0,2},{1,3},{2,0},{3,1},{4,6},{5,7},{6,4},{7,5},{8,10},{9,11},{10,... | collective-permute-start | bytes 393224 | tf_op jit(solution)/shard_map/ppermute | solution.py:588
  247.8 10.5 %collective-permute-start.48 = (bf16[64,512]{1,0:T(8,128)(2,1)S(1)}, bf16[64,512]{1,0:T(8,128)(2,1)S(1)}, u32[]{:S(2)}, u32[]{:S(2)}) collective-permute-start(bf16[64,512]{1,0:T(8,128)(2,1)S(1)} %get-tuple-element.353), channel_id=1, source_target_pairs={{0,2},{1,3},{2,0},{3,1},{4,6},{5,7},{6,4},{7,5},{8,10},{9,11},{10,... | collective-permute-start | bytes 196616 | tf_op jit(solution)/shard_map/ppermute | solution.py:588
  248.0 10.3 %collective-permute-start.49 = (bf16[64,512]{1,0:T(8,128)(2,1)S(1)}, bf16[64,512]{1,0:T(8,128)(2,1)S(1)}, u32[]{:S(2)}, u32[]{:S(2)}) collective-permute-start(bf16[64,512]{1,0:T(8,128)(2,1)S(1)} %get-tuple-element.352), channel_id=1, source_target_pairs={{0,4},{1,5},{2,6},{3,7},{4,0},{5,1},{6,2},{7,3},{8,12},{9,13},{10,... | collective-permute-start | bytes 196616 | tf_op jit(solution)/shard_map/ppermute | solution.py:588
  274.8 11.1 %collective-permute-start.54 = (bf16[64,1024]{1,0:T(8,128)(2,1)S(1)}, bf16[64,1024]{1,0:T(8,128)(2,1)S(1)}, u32[]{:S(2)}, u32[]{:S(2)}) collective-permute-start(bf16[64,1024]{1,0:T(8,128)(2,1)S(1)} %get-tuple-element.347), channel_id=1, source_target_pairs={{0,12},{1,13},{2,14},{3,15},{4,8},{5,9},{6,10},{7,11},{8,20},{9,21... | collective-permute-start | bytes 393224 | tf_op jit(solution)/shard_map/ppermute | solution.py:599
  275.9 10.0 %collective-permute-start.55 = (bf16[64,1024]{1,0:T(8,128)(2,1)S(1)}, bf16[64,1024]{1,0:T(8,128)(2,1)S(1)}, u32[]{:S(2)}, u32[]{:S(2)}) collective-permute-start(bf16[64,1024]{1,0:T(8,128)(2,1)S(1)} %get-tuple-element.348), channel_id=1, source_target_pairs={{0,8},{1,9},{2,10},{3,11},{4,12},{5,13},{6,14},{7,15},{8,16},{9,17... | collective-permute-start | bytes 393224 | tf_op jit(solution)/shard_map/ppermute | solution.py:599
  (28 other events, 235.1 us)
